TPU v7x, 32 devices: a whole 2x2x4 slice. The times are simulated.
32 devices in a mesh: row: 8 (over y, x, core), col: 4 (over z).
Axes of the slice: x: 2, y: 2, z: 4, core: 2. Of those that a mesh axis runs over, the one named last changes fastest.
Arguments:
- frame_first: float32 [4, 2048, 1024], P(None, 'row', 'col'), may hold values from -10 to 10
- frame_second: float32 [4, 2048, 1024], P(None, 'row', 'col'), may hold values from -10 to 10
- shifts: int32 [8, 4, 2], P('row', 'col'), may hold values from -4 to 4, as said below
Outputs:
- flow_field: float32 [2, 2048, 1024], P(None, 'row', 'col')
- coarse_flow: float32 [2, 256, 128], P(None, 'row', 'col')
Inputs may be any that keep to these rules, and one draw needn't show every extreme that they name: `shifts`: some tile has displacement 4 along rows and some tile -4 along columns.
All inputs are finite; a program needn't handle non-finite values.
Results may differ from a plain program's by a relative error of at most 0.0003.
Values sent between devices are 32-bit elements; how exact they have to be, the bound alone decides.
No kernel may reach another device: no remote copies, remote signals or barrier semaphores. Data moves between devices by JAX's collectives and lax.ppermute only.
A program may use at most 64 MiB of HBM per device.

v0:
```python
import functools

import jax
import jax.numpy as jnp
from jax import lax
from jax.experimental import pallas as pl
from jax.experimental.pallas import tpu as pltpu
from jax.sharding import PartitionSpec as P

FACTOR = 8
MAXD = 4
BANDS = 4
STEPS = 3
LANES = 128
COLUMNS = 2 * LANES
HALF = 64
SUB = 8
DEPTH = 4
REACH = DEPTH + MAXD + 1
SLOT = 16
C_SECOND = 6
C_FIRST = 5
LEAD = 8
MARGIN = 48
EDGE = 46
GUARD = 8
HALO = 8
BEGIN = 40
EACH = MARGIN + 16
LIMIT = 0.3
ALPHA = 0.3
UNIT = 0.125 / ALPHA

S_MID = 55
S_RIGHT = 110
S_LEFT = LANES - REACH
S_TURN = COLUMNS - S_RIGHT - LANES

E8 = 0
H8 = 64
E1 = 72
H1 = 80
META = 81
F4 = 88
CS = 120
ROW_MESSAGE = 144
H_BAND = 32

COARSE_A = REACH + DEPTH
COARSE_B = SLOT + REACH + DEPTH
SHIFT_R = 2 * SLOT + REACH + DEPTH
SHIFT_C = SHIFT_R + 1
EXISTS = SHIFT_R + 2


def lanes_of(rows=SUB):
    return lax.broadcasted_iota(jnp.int32, (rows, LANES), 1)


def lanes_like(x):
    return lax.broadcasted_iota(jnp.int32, x.shape, 1)


def turn(x, amount):
    amount = amount % LANES
    return x if amount == 0 else pltpu.roll(x, amount, 1)


def turn_back(x, shift):
    return pltpu.roll(x, lax.rem(LANES - shift, LANES), 1)


def split_dot(x, exact):
    high = x.astype(jnp.bfloat16)
    rest = x - high.astype(jnp.float32)
    middle = rest.astype(jnp.bfloat16)
    low = (rest - middle.astype(jnp.float32)).astype(jnp.bfloat16)
    parts = [jnp.dot(part, exact, preferred_element_type=jnp.float32) for part in (low, middle, high)]
    return parts[0] + parts[1] + parts[2]


def scalar_at(ref, row, lane):
    return ref[row : row + 1, lane : lane + 1][0, 0]


def int_at(ref, row, lane):
    return scalar_at(ref, row, lane).astype(jnp.int32)


def is_even(axis, like):
    return jnp.broadcast_to(lax.axis_index(axis) % 2, like.shape) == 0


def without_ends(message, axis, count):
    place = jnp.broadcast_to(lax.axis_index(axis), message.shape)
    return jnp.where((place > 0) & (place < count - 1), message[...], 0.0)


def staggered(items, compute, store, depth, woven=None):
    pending = []
    for item in items:
        pending.append((item, compute(item)))
        if woven is not None:
            woven.advance()
        if len(pending) > depth:
            store(*pending.pop(0))
    for entry in pending:
        store(*entry)


class Woven:
    def __init__(self, stages):
        self.stages = stages
        self.result = None

    def advance(self):
        try:
            next(self.stages)
            return True
        except StopIteration as end:
            self.result = end.value if self.result is None else self.result
            return False

    def finish(self):
        while self.advance():
            pass
        return self.result


def pack_image(packed, to_right, planes, count, offset):
    bands, height, _ = planes[0].shape
    plane = planes[int(to_right)]
    start = LANES - count if to_right else 0
    length = height // 2
    lane = lanes_of(length)
    for half in range(2):
        for band in range(bands):
            at = half * HALF + band * SLOT + offset
            cells = turn(plane[band, half * length : (half + 1) * length, :], at - start)
            packed = cells if packed is None else jnp.where((lane >= at) & (lane < at + count), cells, packed)
    return packed


def pack_means(packed, to_right, means):
    length = packed.shape[0]
    start = LEAD + COLUMNS // FACTOR - C_SECOND if to_right else LEAD
    lane = lanes_of(length)
    for half in range(2):
        cells = means[half * length : (half + 1) * length]
        for at, first in ((half * HALF + COARSE_A, start), (half * HALF + COARSE_B, start + 3)):
            packed = jnp.where((lane >= at) & (lane < at + 3), turn(cells, at - first), packed)
    return packed


def column_meta(message):
    return (int_at(message, 0, SHIFT_R), int_at(message, 0, SHIFT_C)), scalar_at(message, 0, EXISTS)


def strip_second(base, from_left, from_right, rows, half, band):
    at = half * HALF + band * SLOT
    lane = lanes_like(base)
    cells = jnp.where(lane >= S_RIGHT, turn(from_right[rows, :], S_RIGHT - at), base)
    return jnp.where(lane >= S_LEFT, turn(from_left[rows, :], S_LEFT - at), cells)


def strip_first(base, from_left, from_right, rows, half, band):
    at = half * HALF + band * SLOT + REACH
    lane = lanes_like(base)
    cells = jnp.where(lane >= S_RIGHT, turn(from_right[rows, :], S_RIGHT - at), base)
    return jnp.where(lane >= S_LEFT, turn(from_left[rows, :], LANES - DEPTH - at), cells)


def strip_halo(base, beside, band, start, count):
    at = band * H_BAND + start
    lane = lanes_like(base)
    cells = jnp.where(lane >= S_RIGHT, turn(beside, S_RIGHT - at), base)
    return jnp.where(lane >= S_LEFT, turn(beside, LANES - count - at - SLOT), cells)


def strip_own(planes):
    return jnp.where(lanes_like(planes[0]) < S_MID, planes[0], turn(planes[1], -S_TURN))


def first_kernel(
    second_hbm, first_hbm, shifts_hbm, second_0, second_1, first_0, first_1, coarse, swap_0, swap_1, own_meta,
    shifts, sems, shift_sem,
):
    seconds, firsts = (second_0, second_1), (first_0, first_1)
    bands, height, _ = second_0.shape
    width = COLUMNS
    coarse_height = height // FACTOR
    lane = lanes_of()
    get_shifts = pltpu.make_async_copy(shifts_hbm, shifts, shift_sem)
    get_shifts.start()
    copies = []
    for image, (source, refs) in enumerate(((second_hbm, seconds), (first_hbm, firsts))):
        for band in range(bands):
            for tile, ref in enumerate(refs):
                copy = pltpu.make_async_copy(
                    source.at[band, :, pl.ds(tile * LANES, LANES)], ref.at[band], sems.at[image, band, tile]
                )
                copy.start()
                copies.append((image * bands + band, tile, ref, band, copy))
    cell = lax.broadcasted_iota(jnp.int32, (width, LANES), 0)
    place = lax.broadcasted_iota(jnp.int32, (width, LANES), 1)
    weights = jnp.where(place - LEAD == cell // FACTOR, 1.0 / (FACTOR * FACTOR), 0.0).astype(jnp.bfloat16)
    means = []
    packed = [None, None]
    for image, (count, offset) in enumerate(((REACH, 0), (DEPTH, REACH))):
        group = copies[image * 2 * bands : (image + 1) * 2 * bands]
        sums = {}
        for *_, copy in group:
            copy.wait()
        for plane, tile, ref, band, _ in group:
            parts = [ref[band, pl.ds(k, coarse_height, stride=FACTOR), :] for k in range(FACTOR)]
            while len(parts) > 1:
                parts = [x + y for x, y in zip(parts[::2], parts[1::2])]
            sums[plane, tile] = parts[0]
        tall = [jnp.concatenate([sums[image * bands + band, tile] for tile in range(2)], axis=1) for band in range(bands)]
        means.append(split_dot(jnp.concatenate(tall, axis=0), weights))
        packed = [
            pack_image(packed[side], bool(side), (seconds, firsts)[image], count, offset) for side in range(2)
        ]
    means = jnp.concatenate(means, axis=0)
    get_shifts.wait()
    shift_rows = shifts[0, 0, 0].astype(jnp.float32)
    shift_cols = shifts[0, 0, 1].astype(jnp.float32)
    place = lanes_of(height // 2) & (HALF - 1)
    packed = [
        jnp.where(place == SHIFT_R, shift_rows, jnp.where(place == SHIFT_C, shift_cols, jnp.where(place == EXISTS, 1.0, x)))
        for x in packed
    ]
    to_left, to_right = [pack_means(packed[side], bool(side), means) for side in range(2)]
    coarse[...] = means
    own_meta[...] = jnp.where(lane < HALF, shift_rows, shift_cols)
    even = is_even("col", swap_0)
    swap_0[...] = jnp.where(even, to_right, to_left)
    swap_1[...] = jnp.where(even, to_left, to_right)


def message_kernel(
    count, coarse, own_meta, got_0, got_1, up_part, down_part, _whole, swap_0, swap_1, from_left, from_right, wide
):
    other = without_ends(got_1, "col", count)
    even = is_even("col", got_0)
    from_right[...] = jnp.where(even, got_0[...], other)
    from_left[...] = jnp.where(even, other, got_0[...])
    planes_coarse, coarse_height, _ = wide.shape
    bands = planes_coarse // 2
    end = from_left.shape[0]
    coarse_width = COLUMNS // FACTOR
    lane = lanes_of()
    wides = []
    for plane in range(planes_coarse):
        half, block = divmod(plane, planes_coarse // 2)
        for step in range(coarse_height // SUB):
            own = slice(plane * coarse_height + step * SUB, plane * coarse_height + (step + 1) * SUB)
            rows = slice(block * coarse_height + step * SUB, block * coarse_height + (step + 1) * SUB)
            at = half * HALF
            left = from_left[rows, :]
            right = from_right[rows, :]
            start = LEAD - C_SECOND
            cells = turn(left, start - at - COARSE_A)
            cells = jnp.where(lane >= start + 3, turn(left, start + 3 - at - COARSE_B), cells)
            cells = jnp.where(lane >= LEAD, coarse[own, :], cells)
            start = LEAD + coarse_width
            cells = jnp.where(lane >= start, turn(right, start - at - COARSE_A), cells)
            cells = jnp.where(lane >= start + 3, turn(right, start + 3 - at - COARSE_B), cells)
            wides.append((plane, step, cells))
    for plane, step, cells in wides:
        wide[plane, step * SUB : (step + 1) * SUB, :] = cells
    row = lax.broadcasted_iota(jnp.int32, (SUB, LANES), 0)
    meta = jnp.where(lane < 16, own_meta[...], jnp.where(lane < 32, turn(own_meta[...], HALF), 1.0))
    for message, at in ((from_left, 48), (from_right, 80)):
        first_rows = message[0:SUB, :]
        rows = jnp.broadcast_to(first_rows[:, SHIFT_R : SHIFT_R + 1], (SUB, LANES))
        cols = jnp.broadcast_to(first_rows[:, SHIFT_C : SHIFT_C + 1], (SUB, LANES))
        meta = jnp.where(lane >= at, rows, meta)
        meta = jnp.where(lane >= at + 16, cols, meta)

    def beside(rows, half):
        left = from_left[rows, :]
        right = from_right[rows, :]
        cells = jnp.zeros((SUB, LANES), jnp.float32)
        for band in range(bands):
            at = half * HALF + band * SLOT
            cells = jnp.where(lane >= band * H_BAND, turn(right, band * H_BAND - at), cells)
            cells = jnp.where(lane >= band * H_BAND + SLOT, turn(left, band * H_BAND + SLOT - at), cells)
        return cells

    even = is_even("row", meta)
    parts = []
    for part, half, near, next_rows, row_of in (
        (up_part, 0, slice(0, 8), slice(8, 16), 0),
        (down_part, 1, slice(end - 8, end), slice(end - 16, end - 8), 7),
    ):
        eight = beside(near, half)
        one = beside(next_rows, half)
        one = jnp.broadcast_to(one[row_of : row_of + 1], (SUB, LANES))
        coarse_rows = []
        for band in range(bands):
            rows = slice(0, C_SECOND) if half == 0 else slice(coarse_height - C_SECOND, coarse_height)
            second = wide[band, rows, :]
            first = turn(wide[bands + band, rows, :], HALF)
            coarse_rows.append(jnp.where(lanes_like(second) < HALF, second, first))
        parts.append([
            (part[E8:H8, :], E8), (eight, H8), (part[E1:H1, :], E1), (jnp.where(row == 0, one, meta), H1),
            (part[F4:CS, :], F4), *[(x, CS + k * C_SECOND) for k, x in enumerate(coarse_rows)],
        ])
    for (up, at), (down, _) in zip(*parts):
        even = is_even("row", up)
        swap_0[at : at + up.shape[0], :] = jnp.where(even, down, up)
        swap_1[at : at + up.shape[0], :] = jnp.where(even, up, down)


def coarse_flow_of(second, first, mask):
    def along_rows(x):
        return pltpu.roll(x, x.shape[0] - 1, 0) - pltpu.roll(x, 1, 0)

    def along_cols(x):
        return pltpu.roll(x, LANES - 1, 1) - pltpu.roll(x, 1, 1)

    bands = BANDS
    size = second.shape[0] // bands
    grad_rows = 0.125 * along_rows(second)
    grad_cols = 0.125 * along_cols(second)
    offset = 0.25 * (second - first)
    data = jnp.clip(offset, -LIMIT, LIMIT)
    yield

    def pull(grads):
        terms = data * grads
        return sum(terms[k * size : (k + 1) * size] for k in range(bands))

    def tall(x):
        return jnp.concatenate([x] * bands, axis=0)

    flow = [-mask * pull(grad_rows), -mask * pull(grad_cols)]
    extrapolated = [2.0 * x for x in flow]
    dual_rows = [0.0, 0.0]
    dual_cols = [0.0, 0.0]
    yield
    for step in range(1, STEPS):
        changes = [(along_rows(x), along_cols(x)) for x in extrapolated]
        yield
        data = data + offset + grad_rows * tall(extrapolated[0]) + grad_cols * tall(extrapolated[1])
        data = jnp.clip(data, -LIMIT, LIMIT)
        yield
        for c in range(2):
            rows = dual_rows[c] + changes[c][0]
            cols = dual_cols[c] + changes[c][1]
            scale = jnp.minimum(mask, (8.0 * ALPHA) * lax.rsqrt(rows * rows + cols * cols))
            dual_rows[c] = rows * scale
            dual_cols[c] = cols * scale
        yield
        divergences = [along_rows(dual_rows[c]) + along_cols(dual_cols[c]) for c in range(2)]
        yield
        pulls = [pull(grad_rows), pull(grad_cols)]
        yield
        for c in range(2):
            following = flow[c] + mask * ((1.0 / 64.0) * divergences[c] - pulls[c])
            extrapolated[c] = 2.0 * following - flow[c]
            flow[c] = following
        yield
    return flow


def columns_of_planes(planes):
    whole = lax.broadcasted_iota(jnp.int32, (LANES, COLUMNS), 1)
    lane = lax.broadcasted_iota(jnp.int32, (LANES, LANES), 1)
    strip = jnp.where(lane < S_MID, lane, jnp.where(lane < S_LEFT, lane + (COLUMNS - S_RIGHT), lane - LANES))
    return jnp.concatenate([x for x, wanted in ((whole, "whole"), (strip, "strip")) if wanted in planes], axis=1)


def upsample(flow, planes, target):
    column = columns_of_planes(planes)
    source = lax.broadcasted_iota(jnp.int32, column.shape, 0)
    spread = jnp.where(source - LEAD == lax.shift_right_arithmetic(column, 3), float(FACTOR), 0.0).astype(jnp.bfloat16)
    rows = flow[0].shape[0]
    wide = split_dot(UNIT * jnp.concatenate(flow, axis=0), spread)
    for c in range(2):
        for tile in range(column.shape[1] // LANES):
            target[c, tile] = wide[c * rows : (c + 1) * rows, tile * LANES : (tile + 1) * LANES]


def repeat_rows(spread, initial, cells):
    for c in range(2):
        for tile in range(initial.shape[1]):
            rows = [jnp.broadcast_to(spread[c, tile, cell : cell + 1, :], (SUB, LANES)) for cell in cells]
            initial[c, tile, GUARD : GUARD + SUB * len(cells), :] = jnp.concatenate(rows, axis=0)


def shift_whole(here, shift):
    turned = [turn_back(x, shift) for x in here]
    lane = lanes_like(here[0])
    return [
        jnp.where(lane + shift >= LANES, turned[1], turned[0]),
        jnp.where(lane + shift < 0, turned[0], turned[1]),
    ]


def edge_lanes(rows):
    lane = lanes_of(rows)
    return lane == LANES - 1, lane == 0


def columns_whole(fields, edges):
    rows = fields[0].shape[0]
    if rows not in edges:
        edges[rows] = edge_lanes(rows)
    last, first = edges[rows]
    ahead = [pltpu.roll(x, LANES - 1, 1) for x in fields]
    behind = [pltpu.roll(x, 1, 1) for x in fields]
    return [
        jnp.where(last, ahead[1], ahead[0]) - behind[0],
        ahead[1] - jnp.where(first, behind[0], behind[1]),
    ]


def rows_within(tall):
    size = tall.shape[0]
    return (pltpu.roll(tall, size - 1, 0) - pltpu.roll(tall, 1, 0))[SUB : size - SUB]


def columns_strip(field):
    return pltpu.roll(field, LANES - 1, 1) - pltpu.roll(field, 1, 1)


def strip_windows(window, centre, right, left):
    own = turn_back(window(centre[0]), centre[1])
    beyond_left = turn_back(window(left[0]), left[1])
    beyond_right = turn_back(window(right[0]), right[1])
    lane = lanes_like(own)
    beyond = jnp.where((lane >= S_LEFT) | (lane < S_MID), beyond_left, beyond_right)
    is_beyond = lane >= S_RIGHT
    of_next = is_beyond & (lane != S_RIGHT) | (lane == 0)
    of_previous = is_beyond & (lane != LANES - 1) | (lane == S_RIGHT - 1)
    change = turn(jnp.where(of_next, beyond, own), -1) - turn(jnp.where(of_previous, beyond, own), 1)
    return jnp.where(is_beyond, beyond, own), change


def fine_steps(
    rows_total, chunk, columns, initial, extrap, dual_rows, dual_cols, change, dual_data,
    offsets, grads_rows, grads_cols, data_row, masks_of, result, kept, done=lambda k: None,
):
    assert STEPS == 3
    planes = len(offsets)
    bands = offsets[0].shape[0]
    chunks = rows_total // chunk

    def places(k, trim=(0, 0)):
        start, size = k * chunk + trim[0], chunk - sum(trim)
        return pl.ds(GUARD + start, size), pl.ds(start, size), pl.ds(data_row(k) + trim[0], size)

    def row_change(ref, c, tile, at):
        return ref[c, tile, pl.ds(at.start + 1, at.size), :] - ref[c, tile, pl.ds(at.start - 1, at.size), :]

    def clip(x):
        return jnp.clip(x, -UNIT * LIMIT, UNIT * LIMIT)

    tiles = range(planes)

    for step in range(STEPS):
        source = initial if step == 0 else extrap
        final = step == STEPS - 1

        def dual(item, source=source, step=step):
            k, c = item
            at, own, _ = places(k)
            masks = masks_of(own)
            along = columns([source[c, tile, at, :] for tile in tiles])
            values = []
            for tile in tiles:
                rows = row_change(source, c, tile, at)
                cols = along[tile]
                if step > 0:
                    rows = rows + dual_rows[c, tile, at, :]
                    cols = cols + dual_cols[c, tile, own, :]
                scale = jnp.minimum(masks[tile], lax.rsqrt(rows * rows + cols * cols))
                values.append((rows * scale, cols * scale))
            return values

        def store_dual(item, values):
            k, c = item
            for tile, (rows, cols) in enumerate(values):
                dual_rows[c, tile, places(k)[0], :] = rows
                dual_cols[c, tile, places(k)[1], :] = cols

        staggered([(k, c) for k in range(chunks) for c in range(2)], dual, store_dual, 1)
        along_of = {}

        def primal(item, step=step, final=final, along_of=along_of):
            k, tile = item
            at, own, data = places(k, kept(k) if final else (0, 0))
            if k not in along_of:
                along_of[k] = [columns([dual_cols[c, t, own, :] for t in tiles]) for c in range(2)]
            mask = masks_of(own)[tile]
            start = [initial[c, tile, at, :] for c in range(2)]
            if step > 0:
                moved = [extrap[c, tile, at, :] - start[c] for c in range(2)]
            if step == 1:
                changes = [0.5 * x for x in moved]
            if step == 2:
                changes = [change[c, tile, own, :] for c in range(2)]
            pulls = [None, None]
            duals = []
            for band in range(bands):
                gradient = (grads_rows[tile][band, data, :], grads_cols[tile][band, data, :])
                value = offsets[tile][band, data, :]
                if step > 0:
                    earlier = clip(value) if step == 1 else dual_data[band, tile, own, :]
                    value = (value + earlier) + (gradient[0] * moved[0] + gradient[1] * moved[1])
                value = clip(value)
                duals.append(value)
                for c in range(2):
                    term = value * gradient[c]
                    pulls[c] = term if pulls[c] is None else pulls[c] + term
            flows, nexts = [], []
            for c in range(2):
                divergence = row_change(dual_rows, c, tile, at) + along_of[k][c][tile]
                moving = (mask * (1.0 / 64.0)) * divergence - pulls[c]
                total = moving if step == 0 else changes[c] + moving
                flows.append((start[c] + total) * (1.0 / UNIT) if final else total)
                nexts.append(None if final else start[c] + (total + moving))
            return flows, nexts, duals

        def store_primal(item, results, step=step, final=final):
            k, tile = item
            flows, nexts, duals = results
            at, own, _ = places(k, kept(k) if final else (0, 0))
            for c in range(2):
                if final:
                    result[c, tile, own, :] = flows[c]
                else:
                    if step > 0:
                        change[c, tile, own, :] = flows[c]
                    extrap[c, tile, at, :] = nexts[c]
            if final:
                if tile == planes - 1:
                    done(k)
            elif step > 0:
                for band in range(bands):
                    dual_data[band, tile, own, :] = duals[band]

        staggered([(k, tile) for k in range(chunks) for tile in tiles], primal, store_primal, 1)


def clear_guards(*refs):
    for ref in refs:
        rows = ref.shape[2]
        zero = jnp.zeros((GUARD, LANES), jnp.float32)
        for c in range(2):
            for tile in range(ref.shape[1]):
                ref[c, tile, 0:GUARD, :] = zero
                ref[c, tile, rows - GUARD : rows, :] = zero


def fine_scratch(bands, planes, rows):
    guarded = pltpu.VMEM((2, planes, rows + 2 * GUARD, LANES), jnp.float32)
    plain = pltpu.VMEM((2, planes, rows, LANES), jnp.float32)
    return [guarded, guarded, guarded, plain, plain, pltpu.VMEM((bands, planes, rows, LANES), jnp.float32)]


def pieces(bands, height, rows):
    assert (height - 2 * SUB) % rows == 0
    return [(band, row) for row in range(SUB, height - SUB, rows) for band in range(bands)]


def whole_terms_kernel(
    second_0, second_1, first_0, first_1, coarse, own_meta,
    offset, grad_rows, grad_cols, initial, strip_e, strip_f, up, down, moved, spread,
):
    seconds, firsts = (second_0, second_1), (first_0, first_1)
    bands, height, _ = second_0.shape
    block = 120
    coarse_height = coarse.shape[0] // (2 * bands)
    shift_rows, shift_cols = scalar_at(own_meta, 0, 0), scalar_at(own_meta, 0, HALF)
    centre = (shift_rows.astype(jnp.int32), shift_cols.astype(jnp.int32))
    def windows(band, row, rows):
        here = [ref[band, pl.ds(row + centre[0], rows), :].reshape(-1, LANES) for ref in seconds]
        return shift_whole(here, centre[1])

    woven = Woven(coarse_flow_of(coarse[0 : bands * coarse_height, :], coarse[bands * coarse_height :, :], 1.0))

    ends = [(row, windows(slice(None), row, SUB)) for row in (SUB // 2, height - SUB - SUB // 2)]
    for row, values in ends:
        for tile in range(2):
            moved[tile, :, row : row + SUB, :] = values[tile].reshape(bands, SUB, LANES)

    edges = {}

    def values_of(item):
        band, row = item
        values = windows(band, row, block)
        along = columns_whole(values, edges)
        own = [ref[band, row : row + block, :] for ref in firsts]
        return values, [(0.25 * UNIT) * (x - y) for x, y in zip(values, own)], [0.125 * x for x in along]

    def store_values(item, results):
        band, row = item
        values, offsets, gradients = results
        data = slice(row + HALO, row + HALO + block)
        for tile in range(2):
            moved[tile, band, row : row + block, :] = values[tile]
            offset[tile, band, data, :] = offsets[tile]
            grad_cols[tile, band, data, :] = gradients[tile]

    staggered(pieces(bands, height, block), values_of, store_values, 1, woven)

    def strips_of(item):
        band, row = item
        rows = slice(row, row + LANES)
        return strip_own([ref[band, rows, :] for ref in seconds]), strip_own([ref[band, rows, :] for ref in firsts])

    def store_strips(item, results):
        band, row = item
        strip_e[band, row : row + LANES, :], strip_f[band, row : row + LANES, :] = results

    staggered([(band, row) for band in range(bands) for row in range(0, height, LANES)], strips_of, store_strips, 1, woven)

    def gradient_of(item):
        band, row = item
        return [0.125 * rows_within(moved[tile, band, row - SUB : row + 120 + SUB, :]) for tile in range(2)]

    def store_gradient(item, results):
        band, row = item
        for tile in range(2):
            grad_rows[tile, band, row + HALO : row + HALO + 120, :] = results[tile]

    staggered(pieces(bands, height, 120), gradient_of, store_gradient, 1, woven)

    parts = []
    for band in range(bands):
        for second, first in zip(seconds, firsts):
            parts.append((
                second[band, 0:16, :], first[band, 0:8, :],
                second[band, height - 16 : height, :], first[band, height - 8 : height, :],
            ))
    for k, (second_top, first_top, second_end, first_end) in enumerate(parts):
        up[E8 + 8 * k : E8 + 8 * k + 8, :] = second_top[0:8]
        up[E1 + k : E1 + k + 1, :] = second_top[8:9]
        up[F4 + 4 * k : F4 + 4 * k + 4, :] = first_top[0:4]
        down[E8 + 8 * k : E8 + 8 * k + 8, :] = second_end[8:16]
        down[E1 + k : E1 + k + 1, :] = second_end[7:8]
        down[F4 + 4 * k : F4 + 4 * k + 4, :] = first_end[4:8]
    for target in (up, down):
        for start, end in ((H8, E1), (H1, F4), (CS, ROW_MESSAGE)):
            target[start:end, :] = jnp.zeros((end - start, LANES), jnp.float32)

    upsample(woven.finish(), ("whole",), spread)
    clear_guards(initial)
    rows_total = initial.shape[2] - 2 * GUARD
    repeat_rows(spread, initial, [BEGIN // FACTOR + k for k in range(rows_total // SUB)])


def whole_steps_kernel(
    initial, offset, grad_rows, grad_cols, result, extrap, dual_rows, dual_cols, change, dual_data
):
    rows_total = result.shape[2]
    clear_guards(extrap, dual_rows)
    chunk = 88
    edges = {}
    fine_steps(
        rows_total, chunk, lambda fields: columns_whole(fields, edges),
        initial, extrap, dual_rows, dual_cols, change, dual_data,
        *[[ref.at[tile] for tile in range(2)] for ref in (offset, grad_rows, grad_cols)],
        lambda k: HALO + BEGIN + k * chunk, lambda own: (1.0, 1.0), result, lambda k: (SUB * (k == 0), SUB * (k == 1)),
    )


def strip_kernel(
    strip_e, strip_f, from_left, from_right, wide, own_meta, whole,
    middle, strip_out, first_ends, offset, grad_rows, grad_cols,
    moved, result, spread, initial, extrap, dual_rows, dual_cols, change, dual_data,
):
    bands, height, _ = strip_e.shape
    block = 120
    coarse_height = height // FACTOR
    coarse_width = COLUMNS // FACTOR
    rows_total = height - 2 * BEGIN
    lane = lanes_of()
    centre = (int_at(own_meta, 0, 0), int_at(own_meta, 0, HALF))
    right, has_right = column_meta(from_right)
    left, has_left = column_meta(from_left)
    exists = jnp.where(lane < S_RIGHT, 1.0, jnp.where(lane < S_LEFT, has_right, has_left))

    def tall_factor(rows):
        return 0.125 * jnp.concatenate([exists] * (rows // SUB), axis=0)

    mask = jnp.where(lane < LEAD, has_left, jnp.where(lane < LEAD + coarse_width, 1.0, has_right))
    mask = jnp.concatenate([mask] * (coarse_height // SUB), axis=0)
    cells = [wide[k * bands : (k + 1) * bands].reshape(bands * coarse_height, LANES) for k in range(2)]
    woven = Woven(coarse_flow_of(*cells, mask))

    def halves(row, rows):
        half = row // (height // 2)
        start = row - half * (height // 2)
        return half, slice(start, start + rows)

    def second_of(item):
        band, row = item
        half, message = halves(row, LANES)
        return strip_second(strip_e[band, row : row + LANES, :], from_left, from_right, message, half, band)

    def store_second(item, value):
        band, row = item
        strip_out[band, row : row + LANES, :] = value

    staggered([(band, row) for row in range(0, height, LANES) for band in range(bands)], second_of, store_second, 1, woven)

    def first_of(band, row, rows):
        half, message = halves(row, rows)
        return strip_first(strip_f[band, row : row + rows, :], from_left, from_right, message, half, band)

    firsts = [(end, band, first_of(band, (0, height - SUB)[end], SUB)) for end in range(2) for band in range(bands)]
    for end, band, value in firsts:
        first_ends[end, band] = value

    def windows(band, row, rows):
        return strip_windows(
            lambda shift: strip_out[band, pl.ds(row + shift, rows), :].reshape(-1, LANES), centre, right, left
        )

    ends = [(row, windows(slice(None), row, SUB)[0]) for row in (SUB // 2, height - SUB - SUB // 2)]
    for row, value in ends:
        moved[:, row : row + SUB, :] = value.reshape(bands, SUB, LANES)

    factor = tall_factor(block)

    def values_of(item):
        band, row = item
        value, along = windows(band, row, block)
        return value, (0.25 * UNIT) * (value - first_of(band, row, block)), factor * along

    def store_values(item, results):
        band, row = item
        data = slice(row + HALO, row + HALO + block)
        moved[band, row : row + block, :], offset[band, data, :], grad_cols[band, data, :] = results

    staggered(pieces(bands, height, block), values_of, store_values, 1, woven)

    def gradient_of(item):
        band, row = item
        return factor * rows_within(moved[band, row - SUB : row + block + SUB, :])

    def store_gradient(item, value):
        band, row = item
        grad_rows[band, row + HALO : row + HALO + block, :] = value

    staggered(pieces(bands, height, block), gradient_of, store_gradient, 1, woven)

    upsample(woven.finish(), ("strip",), spread)
    clear_guards(initial, extrap, dual_rows)
    repeat_rows(spread, initial, [BEGIN // FACTOR + k for k in range(rows_total // SUB)])

    chunk = 176
    masks = jnp.concatenate([exists] * (chunk // SUB), axis=0)
    fine_steps(
        rows_total, chunk, lambda fields: [columns_strip(fields[0])],
        initial, extrap, dual_rows, dual_cols, change, dual_data, [offset], [grad_rows], [grad_cols],
        lambda k: HALO + BEGIN + k * chunk, lambda own: (masks[: own.size],), result, lambda k: (SUB, SUB),
    )
    join(whole, result.at[:, 0], middle, slice(SUB, rows_total - SUB))


def join(whole, strip, target, rows):
    lane = lanes_of(rows.stop - rows.start)
    values = []
    for c in range(2):
        edge = strip[c, rows, :]
        start = jnp.where(lane < EDGE, edge, whole[c, 0, rows, :])
        values.append((start, jnp.where(lane >= LANES - EDGE, turn(edge, S_TURN), whole[c, 1, rows, :])))
    for c in range(2):
        target[c, rows, 0:LANES], target[c, rows, LANES:COLUMNS] = values[c]


def outer_kernel(
    count, second_0, second_1, first_0, first_1, strip_e, first_ends, from_left, from_right, wide, got_1, got_0, middle, own_meta,
    _wo, _wr, _wc, _so, _sr, _sc,
    flow_out, coarse_out, whole_offset, whole_rows, whole_cols, strip_offset, strip_rows, strip_cols,
    from_up, from_down, extended, tall, spread, masks, result, joined, coarse_result, sems,
    initial, extrap, dual_rows, dual_cols, change, dual_data,
):
    bands, height, _ = second_0.shape
    coarse_height = height // FACTOR
    coarse_width = COLUMNS // FACTOR
    rows_total = 2 * EACH
    lane = lanes_of()

    put_middle = pltpu.make_async_copy(
        middle.at[:, pl.ds(MARGIN - BEGIN, height - 2 * MARGIN), :],
        flow_out.at[:, pl.ds(MARGIN, height - 2 * MARGIN), :],
        sems.at[0],
    )
    put_middle.start()

    other = without_ends(got_1, "row", count)
    even = is_even("row", got_0)
    from_down[...] = jnp.where(even, got_0[...], other)
    from_up[...] = jnp.where(even, other, got_0[...])

    own = (int_at(own_meta, 0, 0), int_at(own_meta, 0, HALF))
    own_right, has_right = column_meta(from_right)
    own_left, has_left = column_meta(from_left)
    has_up = scalar_at(from_up, META, 32)
    has_down = scalar_at(from_down, META, 32)
    exists = jnp.where(lane < S_RIGHT, 1.0, jnp.where(lane < S_LEFT, has_right, has_left))

    def trio(message):
        return (
            (int_at(message, META, 0), int_at(message, META, 16)),
            (int_at(message, META, 80), int_at(message, META, 96)),
            (int_at(message, META, 48), int_at(message, META, 64)),
        )

    above = trio(from_up)
    below = trio(from_down)

    zero = jnp.zeros((SUB, LANES), jnp.float32)
    tall_rows = coarse_height + 2 * LEAD
    parts = []
    fill = jnp.zeros((LEAD - C_SECOND, LANES), jnp.float32)
    for plane in range(2 * bands):
        at = CS + C_SECOND * (plane % bands)
        ends = [turn(message[at : at + C_SECOND, :], HALF * (plane // bands)) for message in (from_up, from_down)]
        parts.append([fill, ends[0], wide[plane], ends[1], fill])
    for plane, values in enumerate(parts):
        tall[plane] = jnp.concatenate(values, axis=0)
    across = jnp.where(lane < LEAD, has_left, jnp.where(lane < LEAD + coarse_width, 1.0, has_right))
    mask = jnp.concatenate([across * has_up] + [across] * (coarse_height // SUB) + [across * has_down], axis=0)
    for end in range(2):
        message = (from_up, from_down)[end]
        beside = message[H8 : H8 + 8, :]
        beside_one = jnp.broadcast_to(message[H1 : H1 + 1, :], (SUB, LANES))
        parts = []
        for band in range(bands):
            eights = [message[E8 + 8 * k : E8 + 8 * k + 8, :] for k in (2 * band, 2 * band + 1)]
            ones = [jnp.broadcast_to(message[E1 + k : E1 + k + 1, :], (SUB, LANES)) for k in (2 * band, 2 * band + 1)]
            eights.append(strip_halo(strip_own(eights), beside, band, 0, REACH))
            ones.append(strip_halo(strip_own(ones), beside_one, band, 0, REACH))
            for tile, (eight, one) in enumerate(zip(eights, ones)):
                source = (second_0, second_1, strip_e)[tile]
                if end == 0:
                    parts.append((tile, band, [one, eight, source[band, 0:24, :]]))
                else:
                    parts.append((tile, band, [source[band, height - 24 : height, :], eight, one]))
        for tile, band, values in parts:
            extended[end, tile, band] = jnp.concatenate(values, axis=0)
    cells = [tall[k * bands : (k + 1) * bands].reshape(bands * tall_rows, LANES) for k in range(2)]
    woven = Woven(coarse_flow_of(*cells, mask))
    edges = {}
    rows_data = whole_offset.shape[2]
    exists_tall = jnp.concatenate([exists] * bands, axis=0)

    def rows_of(halo, end):
        if halo:
            return slice(0, SUB) if end == 0 else slice(rows_data - SUB, rows_data)
        return slice(HALO, HALO + SUB) if end == 0 else slice(rows_data - HALO - SUB, rows_data - HALO)

    def values_of(item):
        halo, end = item
        message = (from_up, from_down)[end]
        base = (SUB, 3 * SUB)[end] if halo else 2 * SUB
        shifts = (above, below)[end] if halo else (own, own_right, own_left)
        factor = 0.125 * (has_up, has_down)[end] if halo else 0.125

        def here(tile, shift):
            return extended[end, tile, :, pl.ds(base + shift, SUB), :].reshape(-1, LANES)

        def down_up(tile, shift):
            return here(tile, shift + 1) - here(tile, shift - 1)

        own_rows = slice(0, SUB) if end == 0 else slice(height - SUB, height)
        if halo:
            firsts = [[], [], []]
            for band in range(bands):
                eights = []
                for k in (2 * band, 2 * band + 1):
                    four = message[F4 + 4 * k : F4 + 4 * k + 4, :]
                    eights.append(jnp.concatenate([four, four], axis=0))
                eights.append(strip_halo(strip_own(eights), message[H8 : H8 + 8, :], band, REACH, DEPTH))
                for tile in range(3):
                    firsts[tile].append(eights[tile])
            firsts = [jnp.concatenate(x, axis=0) for x in firsts]
        else:
            firsts = [x.reshape(-1, LANES) for x in (first_0[:, own_rows, :], first_1[:, own_rows, :], first_ends[end])]
        centre = shifts[0]
        values = shift_whole([here(tile, centre[0]) for tile in range(2)], centre[1])
        changes = shift_whole([down_up(tile, centre[0]) for tile in range(2)], centre[1])
        along = columns_whole(values, edges)
        value, across_cols = strip_windows(lambda shift: here(2, shift), *shifts)
        change_rows, _ = strip_windows(lambda shift: down_up(2, shift), *shifts)
        return (
            [(0.25 * UNIT) * (x - y) for x, y in zip([*values, value], firsts)],
            [*[factor * x for x in changes], (factor * exists_tall) * change_rows],
            [*[factor * x for x in along], (factor * exists_tall) * across_cols],
        )

    def store_values(item, results):
        rows = rows_of(*item)
        for values, whole, strip in zip(
            results, (whole_offset, whole_rows, whole_cols), (strip_offset, strip_rows, strip_cols)
        ):
            values = [x.reshape(bands, SUB, LANES) for x in values]
            for tile in range(2):
                whole[tile, :, rows, :] = values[tile]
            strip[:, rows, :] = values[2]

    staggered([(halo, end) for halo in (True, False) for end in range(2)], values_of, store_values, 1, woven)

    flow = woven.finish()
    for c in range(2):
        coarse_result[c] = turn(flow[c][LEAD : LEAD + coarse_height], -LEAD)[:, :coarse_width]
    put_coarse = pltpu.make_async_copy(coarse_result, coarse_out, sems.at[1])
    put_coarse.start()
    upsample(flow, ("whole", "strip"), spread)
    clear_guards(initial, extrap, dual_rows)
    each = EACH // SUB
    repeat_rows(
        spread, initial,
        [LEAD - 1 + k for k in range(each)] + [tall_rows - LEAD + 1 - each + k for k in range(each)],
    )

    for i, value in enumerate((jnp.ones((SUB, LANES), jnp.float32), exists)):
        masks[i] = jnp.concatenate([value * has_up] + [value] * (rows_total // SUB - 2) + [value * has_down], axis=0)

    def masks_of(rows):
        whole = masks[0, rows, :]
        return (whole, whole, masks[1, rows, :])

    chunk = EACH
    edges = {}
    puts = [
        pltpu.make_async_copy(
            joined.at[:, pl.ds(k * EACH + SUB, MARGIN), :],
            flow_out.at[:, pl.ds(k * (height - MARGIN), MARGIN), :],
            sems.at[2 + k],
        )
        for k in range(2)
    ]

    def finish(k):
        join(result, result.at[:, 2], joined, slice(k * EACH + SUB, k * EACH + SUB + MARGIN))
        puts[k].start()

    def data_row(k):
        return k * (rows_data - EACH)

    fine_steps(
        rows_total, chunk, lambda fields: columns_whole(fields[:2], edges) + [columns_strip(fields[2])],
        initial, extrap, dual_rows, dual_cols, change, dual_data,
        [whole_offset.at[0], whole_offset.at[1], strip_offset],
        [whole_rows.at[0], whole_rows.at[1], strip_rows],
        [whole_cols.at[0], whole_cols.at[1], strip_cols],
        data_row, masks_of, result, lambda k: (SUB, SUB), finish,
    )
    put_middle.wait()
    put_coarse.wait()
    for put in puts:
        put.wait()


def swap_with(message, axis, start):
    names = ("row", "col")
    sizes = [lax.axis_size(name) for name in names]
    along = names.index(axis)
    count, others = sizes[along], sizes[1 - along]

    def number(place, other):
        row, col = (place, other) if along == 0 else (other, place)
        return row * sizes[1] + col

    pairs = [(number(i, k), number(i + 1, k)) for i in range(start, count - 1, 2) for k in range(others)]
    if start and axis == "col":
        pairs += [(number(i, k), number(i, k + 1)) for i in (0, count - 1) for k in range(0, others, 2)]
    elif start:
        pairs += [(number(0, k), number(count - 1, k)) for k in range(others)]
    return lax.ppermute(message, names, pairs + [(j, i) for i, j in pairs])


def local(frame_first, frame_second, shifts):
    bands, height, width = frame_first.shape
    assert bands == 4 and width == COLUMNS and height % LANES == 0
    assert lax.axis_size("row") % 2 == 0 and lax.axis_size("col") % 2 == 0
    coarse_height = height // FACTOR
    coarse_width = width // FACTOR
    vmem = pl.BlockSpec(memory_space=pltpu.VMEM)
    hbm = pl.BlockSpec(memory_space=pltpu.HBM)
    tall_rows = coarse_height + 2 * LEAD
    inner_rows = height - 2 * BEGIN

    def shape(*sizes):
        return jax.ShapeDtypeStruct(sizes, jnp.float32)

    def scratch(*sizes):
        return pltpu.VMEM(sizes, jnp.float32)

    def call(kernel, name, arguments, outs, scratches=(), flops=1_000_000, **more):
        more = {"in_specs": [vmem] * len(arguments), "out_specs": (vmem,) * len(outs), **more}
        return pl.pallas_call(
            kernel,
            out_shape=tuple(outs),
            scratch_shapes=list(scratches),
            compiler_params=pltpu.CompilerParams(vmem_limit_bytes=24 * 1024 * 1024),
            cost_estimate=pl.CostEstimate(flops=flops, bytes_accessed=1_000_000, transcendentals=0),
            name=name,
            **more,
        )(*arguments)

    plane = shape(bands, height, LANES)
    column_message = shape(height // 2, LANES)
    row_message = shape(ROW_MESSAGE, LANES)
    whole_data = shape(2, bands, height + 2 * HALO, LANES)
    strip_data = shape(bands, height + 2 * HALO, LANES)

    *frames, coarse, swap_0, swap_1, own_meta = call(
        first_kernel,
        "means_and_message",
        [pltpu.with_memory_space_constraint(x, pltpu.HBM) for x in (frame_second, frame_first, shifts)],
        [*[plane] * 4, shape(2 * bands * coarse_height, LANES), column_message, column_message, shape(SUB, LANES)],
        [
            pltpu.SMEM((1, 1, 2), jnp.int32),
            pltpu.SemaphoreType.DMA((2, bands, 2)),
            pltpu.SemaphoreType.DMA,
        ],
        in_specs=[hbm] * 3,
    )
    got_0 = swap_with(swap_0, "col", 0)
    got_1 = swap_with(swap_1, "col", 1)

    *whole_terms, initial, strip_e, strip_f, up_part, down_part = call(
        whole_terms_kernel,
        "whole_terms",
        [*frames, coarse, own_meta],
        [
            *[whole_data] * 3, shape(2, 2, inner_rows + 2 * GUARD, LANES),
            plane, plane, row_message, row_message,
        ],
        [scratch(2, bands, height, LANES), scratch(2, 2, coarse_height, LANES)],
        flops=8_000_000,
    )
    (whole,) = call(
        whole_steps_kernel,
        "whole_steps",
        [initial, *whole_terms],
        [shape(2, 2, inner_rows, LANES)],
        fine_scratch(bands, 2, inner_rows)[1:],
        flops=20_000_000,
    )

    swap_0, swap_1, from_left, from_right, wide = call(
        functools.partial(message_kernel, lax.axis_size("col")),
        "row_messages",
        [coarse, own_meta, got_0, got_1, up_part, down_part, whole],
        [row_message, row_message, column_message, column_message, shape(2 * bands, coarse_height, LANES)],
    )
    got_1 = swap_with(swap_1, "row", 1)
    got_0 = swap_with(swap_0, "row", 0)

    middle, strip_e, first_ends, *strip_terms = call(
        strip_kernel,
        "strip",
        [strip_e, strip_f, from_left, from_right, wide, own_meta, whole],
        [shape(2, inner_rows, width), plane, shape(2, bands, SUB, LANES), *[strip_data] * 3],
        [
            scratch(bands, height, LANES),
            scratch(2, 1, inner_rows, LANES),
            scratch(2, 1, coarse_height, LANES),
            *fine_scratch(bands, 1, inner_rows),
        ],
        flops=16_000_000,
    )

    flow, coarse_flow, *_ = call(
        functools.partial(outer_kernel, lax.axis_size("row")),
        "outer_rows",
        [
            *frames, strip_e, first_ends, from_left, from_right, wide, got_1, got_0, middle, own_meta,
            *whole_terms, *strip_terms,
        ],
        [shape(2, height, width), shape(2, coarse_height, coarse_width), *[whole_data] * 3, *[strip_data] * 3],
        [
            scratch(ROW_MESSAGE, LANES),
            scratch(ROW_MESSAGE, LANES),
            scratch(2, 3, bands, 40, LANES),
            scratch(2 * bands, tall_rows, LANES),
            scratch(2, 3, tall_rows, LANES),
            scratch(2, 2 * EACH, LANES),
            scratch(2, 3, 2 * EACH, LANES),
            scratch(2, 2 * EACH, width),
            scratch(2, coarse_height, coarse_width),
            pltpu.SemaphoreType.DMA((4,)),
            *fine_scratch(bands, 3, 2 * EACH),
        ],
        out_specs=(hbm, hbm) + (vmem,) * 6,
        input_output_aliases={13 + k: 2 + k for k in range(6)},
    )
    return (flow, coarse_flow)


def solution(mesh):
    return jax.shard_map(
        local,
        mesh=mesh,
        in_specs=(P(None, "row", "col"), P(None, "row", "col"), P("row", "col", None)),
        out_specs=(P(None, "row", "col"), P(None, "row", "col")),
        check_vma=False,
    )
```

profile of v0, /device:TPU:0, one launch (start us, length us, event | category | flops | bytes accessed | tf_op | source)
XLA Modules:
  0.0 19.7 jit_solution(9052589339175849792)
XLA Ops:
  0.6 2.5 %means_and_message.1 = (f32[4,256,128]{2,1,0:T(8,128)S(1)}, f32[4,256,128]{2,1,0:T(8,128)S(1)}, f32[4,256,128]{2,1,0:T(8,128)S(1)}, f32[4,256,128]{2,1,0:T(8,128...) custom-call(f32[4,256,256]{2,1,0:T(8,128)} %second_hbm.1, ...), custom_call_target="tpu_custom_call" | custom-call | flops 1000000 | bytes 1000000 | tf_op jit(solution)/shard_map/means_and_message/pallas_call | solution.py:1000
  3.1 3.1 %collective-permute-start = (f32[128,128]{1,0:T(8,128)S(1)}, f32[128,128]{1,0:T(8,128)S(1)}, u32[]{:S(2)}, u32[]{:S(2)}) collective-permute-start(f32[128,128]{1,0:T(8,128)S(1)} %get-tuple-element.39), channel_id=1, source_target_pairs={{0,1},{4,5},{8,9},{12,13},{16,17},{20,21},{24,25},{28,29},{2,3},{6... | collective-permute-start | bytes 196616 | tf_op jit(solution)/shard_map/ppermute | solution.py:978
  6.2 0.0 collective-permute-start.1
  6.2 1.8 %whole_terms.1 = (f32[2,4,272,128]{3,2,1,0:T(8,128)S(1)}, f32[2,4,272,128]{3,2,1,0:T(8,128)S(1)}, f32[2,4,272,128]{3,2,1,0:T(8,128)S(1)}, f32[2,2,192,128]{3,2,1...) custom-call(f32[4,256,128]{2,1,0:T(8,128)S(1)} %get-tuple-element.31, ...), custom_call_target="tpu_custom_call" | custom-call | flops 8000000 | bytes 1000000 | tf_op jit(solution)/shard_map/whole_terms/pallas_call | solution.py:1000
  8.0 1.9 %whole_steps.1._whole.whole = f32[2,2,176,128]{3,2,1,0:T(8,128)S(1)} custom-call(f32[2,2,192,128]{3,2,1,0:T(8,128)S(1)} %get-tuple-element.43.initial, f32[2,4,272,128]{3,2,1,0:T(8,128)S(1)} %get-tuple-element.44.offset._wo, f32[2,4,272,128]{3,2,1,0:T(8,128)S(1)} %get-tuple-element.45.grad_rows._wr, f32[2,4,272,128]{3,2,1,0:T(8,128)S(1)} %get-tuple-element.46.grad_cols._wc), custom_call_target="tpu_custom_call" | custom-call | flops 20000000 | bytes 1000000 | tf_op jit(solution)/shard_map/whole_steps/pallas_call | solution.py:1000
  9.9 0.0 collective-permute-done.got_0
  9.9 0.0 collective-permute-done.1.got_1
  9.9 0.3 %row_messages.1 = (f32[144,128]{1,0:T(8,128)S(1)}, f32[144,128]{1,0:T(8,128)S(1)}, f32[128,128]{1,0:T(8,128)S(1)}, f32[128,128]{1,0:T(8,128)S(1)}, f32[8,32,128]{2,1,0:T(8,128)S(1)}) custom-call(f32[256,128]{1,0:T(8,128)S(1)} %get-tuple-element.35.coarse, f32[8,128]{1,0:T(8,128)S(1)} %get-tuple-element.36.own_meta, ...), custom_call_target="tpu_custom_call" | custom-call | flops 1000000 | bytes 1000000 | tf_op jit(solution)/shard_map/row_messages/pallas_call | solution.py:1000
  10.2 2.6 %collective-permute-start.2 = (f32[144,128]{1,0:T(8,128)S(1)}, f32[144,128]{1,0:T(8,128)S(1)}, u32[]{:S(2)}, u32[]{:S(2)}) collective-permute-start(f32[144,128]{1,0:T(8,128)S(1)} %get-tuple-element.52), channel_id=1, source_target_pairs={{4,8},{5,9},{6,10},{7,11},{12,16},{13,17},{14,18},{15,19},{20,24},... | collective-permute-start | bytes 221192 | tf_op jit(solution)/shard_map/ppermute | solution.py:978
  12.8 0.0 collective-permute-start.3
  12.8 2.9 %strip.1 = (f32[2,176,256]{2,1,0:T(8,128)S(1)}, f32[4,256,128]{2,1,0:T(8,128)S(1)}, f32[2,4,8,128]{3,2,1,0:T(8,128)S(1)}, f32[4,272,128]{2,1,0:T(8,128)S(1)}, f3...) custom-call(f32[4,256,128]{2,1,0:T(8,128)S(1)} %get-tuple-element.37.strip_e, ...), custom_call_target="tpu_custom_call" | custom-call | flops 16000000 | bytes 1000000 | tf_op jit(solution)/shard_map/strip/pallas_call | solution.py:1000
  15.7 0.0 collective-permute-done.2.got_1
  15.7 0.0 collective-permute-done.3.got_0
  15.7 4.0 %outer_rows.1 = (f32[2,256,256]{2,1,0:T(8,128)}, f32[2,32,32]{2,1,0:T(8,128)}, f32[2,4,272,128]{3,2,1,0:T(8,128)S(1)}, f32[2,4,272,128]{3,2,1,0:T(8,128)S(1)}, f...) custom-call(f32[4,256,128]{2,1,0:T(8,128)S(1)} %get-tuple-element.31, ...), custom_call_target="tpu_custom_call", output_to_operand_aliasing={{2}: (13, {}), {3}: (14, {}), {4}: (15, {}), {5}: (16, {}),... | custom-call | flops 1000000 | bytes 1000000 | tf_op jit(solution)/shard_map/outer_rows/pallas_call | solution.py:1000
Async XLA Ops:
  3.1 6.8 %collective-permute-start = (f32[128,128]{1,0:T(8,128)S(1)}, f32[128,128]{1,0:T(8,128)S(1)}, u32[]{:S(2)}, u32[]{:S(2)}) collective-permute-start(f32[128,128]{1,0:T(8,128)S(1)} %get-tuple-element.39), channel_id=1, source_target_pairs={{0,1},{4,5},{8,9},{12,13},{16,17},{20,21},{24,25},{28,29},{2,3},{6... | collective-permute-start | bytes 196616 | tf_op jit(solution)/shard_map/ppermute | solution.py:978
  6.2 3.7 %collective-permute-start.1 = (f32[128,128]{1,0:T(8,128)S(1)}, f32[128,128]{1,0:T(8,128)S(1)}, u32[]{:S(2)}, u32[]{:S(2)}) collective-permute-start(f32[128,128]{1,0:T(8,128)S(1)} %get-tuple-element.40), channel_id=1, source_target_pairs={{1,2},{5,6},{9,10},{13,14},{17,18},{21,22},{25,26},{29,30},{0,4},{... | collective-permute-start | bytes 196616 | tf_op jit(solution)/shard_map/ppermute | solution.py:978
  10.2 5.5 %collective-permute-start.2 = (f32[144,128]{1,0:T(8,128)S(1)}, f32[144,128]{1,0:T(8,128)S(1)}, u32[]{:S(2)}, u32[]{:S(2)}) collective-permute-start(f32[144,128]{1,0:T(8,128)S(1)} %get-tuple-element.52), channel_id=1, source_target_pairs={{4,8},{5,9},{6,10},{7,11},{12,16},{13,17},{14,18},{15,19},{20,24},... | collective-permute-start | bytes 221192 | tf_op jit(solution)/shard_map/ppermute | solution.py:978
  12.8 2.9 %collective-permute-start.3 = (f32[144,128]{1,0:T(8,128)S(1)}, f32[144,128]{1,0:T(8,128)S(1)}, u32[]{:S(2)}, u32[]{:S(2)}) collective-permute-start(f32[144,128]{1,0:T(8,128)S(1)} %get-tuple-element.53), channel_id=1, source_target_pairs={{0,4},{1,5},{2,6},{3,7},{8,12},{9,13},{10,14},{11,15},{16,20},{17,... | collective-permute-start | bytes 221192 | tf_op jit(solution)/shard_map/ppermute | solution.py:978
where the time goes:
time: 19.9 us; the launch traced here: 19.7 us
  Pallas kernels  13.3 us (67%)
  starting transfers between devices  5.71 us (29%)
  between operations  0.69 us (3%)
    pallas_call x6, Pallas kernels, call(): pl.pallas_call(kernel, out_shape=tuple(outs), scratch_shapes=list(scratch...  13.3 us
    ppermute x4, starting transfers between devices, swap_with(): return lax.ppermute(message, names, pairs + [(j, i) for i, j in pairs])  5.71 us
  transfers between devices with their start and end apart: 4, of which 0 were waited for; matrix products, arithmetic and copies ran while one was open for 0% of the time, Pallas kernels for 33%

commit v1 on v0

--- a/solution.py
+++ b/solution.py
@@ -79,12 +79,17 @@
     return parts[0] + parts[1] + parts[2]
 
 
-def scalar_at(ref, row, lane):
-    return ref[row : row + 1, lane : lane + 1][0, 0]
-
-
-def int_at(ref, row, lane):
-    return scalar_at(ref, row, lane).astype(jnp.int32)
+def neighbours(axis, count):
+    place = lax.axis_index(axis)
+    return jnp.where(place > 0, 1.0, 0.0), jnp.where(place < count - 1, 1.0, 0.0)
+
+
+def shift_at(numbers, row, lane):
+    return numbers[row, lane].astype(jnp.int32), numbers[row, lane + SLOT].astype(jnp.int32)
+
+
+def shifts_of(numbers):
+    return [shift_at(numbers, META - H1, lane) for lane in (0, 80, 48)]
 
 
 def is_even(axis, like):
@@ -127,14 +132,14 @@
         return self.result
 
 
-def pack_image(packed, to_right, planes, count, offset):
-    bands, height, _ = planes[0].shape
+def pack_image(packed, to_right, planes, some, count, offset):
+    _, height, _ = planes[0].shape
     plane = planes[int(to_right)]
     start = LANES - count if to_right else 0
     length = height // 2
     lane = lanes_of(length)
     for half in range(2):
-        for band in range(bands):
+        for band in some:
             at = half * HALF + band * SLOT + offset
             cells = turn(plane[band, half * length : (half + 1) * length, :], at - start)
             packed = cells if packed is None else jnp.where((lane >= at) & (lane < at + count), cells, packed)
@@ -150,10 +155,6 @@
         for at, first in ((half * HALF + COARSE_A, start), (half * HALF + COARSE_B, start + 3)):
             packed = jnp.where((lane >= at) & (lane < at + 3), turn(cells, at - first), packed)
     return packed
-
-
-def column_meta(message):
-    return (int_at(message, 0, SHIFT_R), int_at(message, 0, SHIFT_C)), scalar_at(message, 0, EXISTS)
 
 
 def strip_second(base, from_left, from_right, rows, half, band):
@@ -207,20 +208,22 @@
     means = []
     packed = [None, None]
     for image, (count, offset) in enumerate(((REACH, 0), (DEPTH, REACH))):
-        group = copies[image * 2 * bands : (image + 1) * 2 * bands]
-        sums = {}
-        for *_, copy in group:
-            copy.wait()
-        for plane, tile, ref, band, _ in group:
-            parts = [ref[band, pl.ds(k, coarse_height, stride=FACTOR), :] for k in range(FACTOR)]
-            while len(parts) > 1:
-                parts = [x + y for x, y in zip(parts[::2], parts[1::2])]
-            sums[plane, tile] = parts[0]
-        tall = [jnp.concatenate([sums[image * bands + band, tile] for tile in range(2)], axis=1) for band in range(bands)]
-        means.append(split_dot(jnp.concatenate(tall, axis=0), weights))
-        packed = [
-            pack_image(packed[side], bool(side), (seconds, firsts)[image], count, offset) for side in range(2)
-        ]
+        for pair in range(0, bands, 2):
+            some = range(pair, pair + 2)
+            group = copies[2 * (image * bands + pair) : 2 * (image * bands + pair + 2)]
+            for *_, copy in group:
+                copy.wait()
+            sums = {}
+            for plane, tile, ref, band, _ in group:
+                parts = [ref[band, pl.ds(k, coarse_height, stride=FACTOR), :] for k in range(FACTOR)]
+                while len(parts) > 1:
+                    parts = [x + y for x, y in zip(parts[::2], parts[1::2])]
+                sums[band, tile] = parts[0]
+            tall = [jnp.concatenate([sums[band, tile] for tile in range(2)], axis=1) for band in some]
+            means.append(split_dot(jnp.concatenate(tall, axis=0), weights))
+            packed = [
+                pack_image(packed[side], bool(side), (seconds, firsts)[image], some, count, offset) for side in range(2)
+            ]
     means = jnp.concatenate(means, axis=0)
     get_shifts.wait()
     shift_rows = shifts[0, 0, 0].astype(jnp.float32)
@@ -232,7 +235,7 @@
     ]
     to_left, to_right = [pack_means(packed[side], bool(side), means) for side in range(2)]
     coarse[...] = means
-    own_meta[...] = jnp.where(lane < HALF, shift_rows, shift_cols)
+    own_meta[...] = jnp.where(lane < SLOT, shift_rows, shift_cols)
     even = is_even("col", swap_0)
     swap_0[...] = jnp.where(even, to_right, to_left)
     swap_1[...] = jnp.where(even, to_left, to_right)
@@ -270,7 +273,7 @@
     for plane, step, cells in wides:
         wide[plane, step * SUB : (step + 1) * SUB, :] = cells
     row = lax.broadcasted_iota(jnp.int32, (SUB, LANES), 0)
-    meta = jnp.where(lane < 16, own_meta[...], jnp.where(lane < 32, turn(own_meta[...], HALF), 1.0))
+    meta = own_meta[...]
     for message, at in ((from_left, 48), (from_right, 80)):
         first_rows = message[0:SUB, :]
         rows = jnp.broadcast_to(first_rows[:, SHIFT_R : SHIFT_R + 1], (SUB, LANES))
@@ -568,19 +571,33 @@
 
 def whole_terms_kernel(
     second_0, second_1, first_0, first_1, coarse, own_meta,
-    offset, grad_rows, grad_cols, initial, strip_e, strip_f, up, down, moved, spread,
+    offset, grad_rows, grad_cols, initial, strip_e, strip_f, up, down, moved, spread, numbers, sem,
 ):
     seconds, firsts = (second_0, second_1), (first_0, first_1)
     bands, height, _ = second_0.shape
     block = 120
     coarse_height = coarse.shape[0] // (2 * bands)
-    shift_rows, shift_cols = scalar_at(own_meta, 0, 0), scalar_at(own_meta, 0, HALF)
-    centre = (shift_rows.astype(jnp.int32), shift_cols.astype(jnp.int32))
+    get_numbers = pltpu.make_async_copy(own_meta, numbers, sem)
+    get_numbers.start()
     def windows(band, row, rows):
         here = [ref[band, pl.ds(row + centre[0], rows), :].reshape(-1, LANES) for ref in seconds]
         return shift_whole(here, centre[1])
 
     woven = Woven(coarse_flow_of(coarse[0 : bands * coarse_height, :], coarse[bands * coarse_height :, :], 1.0))
+
+    def strips_of(item):
+        band, row = item
+        rows = slice(row, row + LANES)
+        return strip_own([ref[band, rows, :] for ref in seconds]), strip_own([ref[band, rows, :] for ref in firsts])
+
+    def store_strips(item, results):
+        band, row = item
+        strip_e[band, row : row + LANES, :], strip_f[band, row : row + LANES, :] = results
+
+    staggered([(band, row) for band in range(bands) for row in range(0, height, LANES)], strips_of, store_strips, 1, woven)
+
+    get_numbers.wait()
+    centre = shift_at(numbers, 0, 0)
 
     ends = [(row, windows(slice(None), row, SUB)) for row in (SUB // 2, height - SUB - SUB // 2)]
     for row, values in ends:
@@ -606,17 +623,6 @@
             grad_cols[tile, band, data, :] = gradients[tile]
 
     staggered(pieces(bands, height, block), values_of, store_values, 1, woven)
-
-    def strips_of(item):
-        band, row = item
-        rows = slice(row, row + LANES)
-        return strip_own([ref[band, rows, :] for ref in seconds]), strip_own([ref[band, rows, :] for ref in firsts])
-
-    def store_strips(item, results):
-        band, row = item
-        strip_e[band, row : row + LANES, :], strip_f[band, row : row + LANES, :] = results
-
-    staggered([(band, row) for band in range(bands) for row in range(0, height, LANES)], strips_of, store_strips, 1, woven)
 
     def gradient_of(item):
         band, row = item
@@ -669,9 +675,9 @@
 
 
 def strip_kernel(
-    strip_e, strip_f, from_left, from_right, wide, own_meta, whole,
+    count, strip_e, strip_f, from_left, from_right, wide, own_message, whole,
     middle, strip_out, first_ends, offset, grad_rows, grad_cols,
-    moved, result, spread, initial, extrap, dual_rows, dual_cols, change, dual_data,
+    moved, result, spread, numbers, sem, initial, extrap, dual_rows, dual_cols, change, dual_data,
 ):
     bands, height, _ = strip_e.shape
     block = 120
@@ -679,9 +685,9 @@
     coarse_width = COLUMNS // FACTOR
     rows_total = height - 2 * BEGIN
     lane = lanes_of()
-    centre = (int_at(own_meta, 0, 0), int_at(own_meta, 0, HALF))
-    right, has_right = column_meta(from_right)
-    left, has_left = column_meta(from_left)
+    get_numbers = pltpu.make_async_copy(own_message.at[pl.ds(H1, SUB), :], numbers, sem)
+    get_numbers.start()
+    has_left, has_right = neighbours("col", count)
     exists = jnp.where(lane < S_RIGHT, 1.0, jnp.where(lane < S_LEFT, has_right, has_left))
 
     def tall_factor(rows):
@@ -715,6 +721,9 @@
     firsts = [(end, band, first_of(band, (0, height - SUB)[end], SUB)) for end in range(2) for band in range(bands)]
     for end, band, value in firsts:
         first_ends[end, band] = value
+
+    get_numbers.wait()
+    centre, right, left = shifts_of(numbers)
 
     def windows(band, row, rows):
         return strip_windows(
@@ -775,10 +784,10 @@
 
 
 def outer_kernel(
-    count, second_0, second_1, first_0, first_1, strip_e, first_ends, from_left, from_right, wide, got_1, got_0, middle, own_meta,
+    counts, second_0, second_1, first_0, first_1, strip_e, first_ends, wide, got_1, got_0, middle, own_message,
     _wo, _wr, _wc, _so, _sr, _sc,
     flow_out, coarse_out, whole_offset, whole_rows, whole_cols, strip_offset, strip_rows, strip_cols,
-    from_up, from_down, extended, tall, spread, masks, result, joined, coarse_result, sems,
+    from_up, from_down, extended, tall, spread, masks, result, joined, coarse_result, numbers, sems,
     initial, extrap, dual_rows, dual_cols, change, dual_data,
 ):
     bands, height, _ = second_0.shape
@@ -793,28 +802,21 @@
         sems.at[0],
     )
     put_middle.start()
-
-    other = without_ends(got_1, "row", count)
+    get_numbers = [
+        pltpu.make_async_copy(message.at[pl.ds(H1, SUB), :], numbers.at[k], sems.at[4 + k])
+        for k, message in enumerate((own_message, got_0, got_1))
+    ]
+    for get in get_numbers:
+        get.start()
+
+    other = without_ends(got_1, "row", counts[0])
     even = is_even("row", got_0)
     from_down[...] = jnp.where(even, got_0[...], other)
     from_up[...] = jnp.where(even, other, got_0[...])
 
-    own = (int_at(own_meta, 0, 0), int_at(own_meta, 0, HALF))
-    own_right, has_right = column_meta(from_right)
-    own_left, has_left = column_meta(from_left)
-    has_up = scalar_at(from_up, META, 32)
-    has_down = scalar_at(from_down, META, 32)
+    has_up, has_down = neighbours("row", counts[0])
+    has_left, has_right = neighbours("col", counts[1])
     exists = jnp.where(lane < S_RIGHT, 1.0, jnp.where(lane < S_LEFT, has_right, has_left))
-
-    def trio(message):
-        return (
-            (int_at(message, META, 0), int_at(message, META, 16)),
-            (int_at(message, META, 80), int_at(message, META, 96)),
-            (int_at(message, META, 48), int_at(message, META, 64)),
-        )
-
-    above = trio(from_up)
-    below = trio(from_down)
 
     zero = jnp.zeros((SUB, LANES), jnp.float32)
     tall_rows = coarse_height + 2 * LEAD
@@ -852,6 +854,16 @@
     rows_data = whole_offset.shape[2]
     exists_tall = jnp.concatenate([exists] * bands, axis=0)
 
+    for get in get_numbers:
+        get.wait()
+    own, one, other = [shifts_of(numbers.at[k]) for k in range(3)]
+    odd = lax.axis_index("row") % 2
+
+    def of_row(for_even, for_odd):
+        return [tuple(jnp.where(odd == 0, x, y) for x, y in zip(*pair)) for pair in zip(for_even, for_odd)]
+
+    above, below = of_row(other, one), of_row(one, other)
+
     def rows_of(halo, end):
         if halo:
             return slice(0, SUB) if end == 0 else slice(rows_data - SUB, rows_data)
@@ -861,7 +873,7 @@
         halo, end = item
         message = (from_up, from_down)[end]
         base = (SUB, 3 * SUB)[end] if halo else 2 * SUB
-        shifts = (above, below)[end] if halo else (own, own_right, own_left)
+        shifts = (above, below)[end] if halo else own
         factor = 0.125 * (has_up, has_down)[end] if halo else 0.125
 
         def here(tile, shift):
@@ -1036,7 +1048,10 @@
             *[whole_data] * 3, shape(2, 2, inner_rows + 2 * GUARD, LANES),
             plane, plane, row_message, row_message,
         ],
-        [scratch(2, bands, height, LANES), scratch(2, 2, coarse_height, LANES)],
+        [
+            scratch(2, bands, height, LANES), scratch(2, 2, coarse_height, LANES),
+            pltpu.SMEM((SUB, LANES), jnp.float32), pltpu.SemaphoreType.DMA,
+        ],
         flops=8_000_000,
     )
     (whole,) = call(
@@ -1058,24 +1073,26 @@
     got_0 = swap_with(swap_0, "row", 0)
 
     middle, strip_e, first_ends, *strip_terms = call(
-        strip_kernel,
+        functools.partial(strip_kernel, lax.axis_size("col")),
         "strip",
-        [strip_e, strip_f, from_left, from_right, wide, own_meta, whole],
+        [strip_e, strip_f, from_left, from_right, wide, swap_0, whole],
         [shape(2, inner_rows, width), plane, shape(2, bands, SUB, LANES), *[strip_data] * 3],
         [
             scratch(bands, height, LANES),
             scratch(2, 1, inner_rows, LANES),
             scratch(2, 1, coarse_height, LANES),
+            pltpu.SMEM((SUB, LANES), jnp.float32),
+            pltpu.SemaphoreType.DMA,
             *fine_scratch(bands, 1, inner_rows),
         ],
         flops=16_000_000,
     )
 
     flow, coarse_flow, *_ = call(
-        functools.partial(outer_kernel, lax.axis_size("row")),
+        functools.partial(outer_kernel, (lax.axis_size("row"), lax.axis_size("col"))),
         "outer_rows",
         [
-            *frames, strip_e, first_ends, from_left, from_right, wide, got_1, got_0, middle, own_meta,
+            *frames, strip_e, first_ends, wide, got_1, got_0, middle, swap_0,
             *whole_terms, *strip_terms,
         ],
         [shape(2, height, width), shape(2, coarse_height, coarse_width), *[whole_data] * 3, *[strip_data] * 3],
@@ -1089,11 +1106,12 @@
             scratch(2, 3, 2 * EACH, LANES),
             scratch(2, 2 * EACH, width),
             scratch(2, coarse_height, coarse_width),
-            pltpu.SemaphoreType.DMA((4,)),
+            pltpu.SMEM((3, SUB, LANES), jnp.float32),
+            pltpu.SemaphoreType.DMA((7,)),
             *fine_scratch(bands, 3, 2 * EACH),
         ],
         out_specs=(hbm, hbm) + (vmem,) * 6,
-        input_output_aliases={13 + k: 2 + k for k in range(6)},
+        input_output_aliases={11 + k: 2 + k for k in range(6)},
     )
     return (flow, coarse_flow)
 

time: 19.9 us -> 21.3 us (1.070)
  Pallas kernels: 13.3 us -> 14.7 us
    pallas_call x6, Pallas kernels: 13.3 us -> 14.7 us  [call(): pl.pallas_call(kernel, out_shape=tuple(outs), scratch_shapes=list(scratch...]
  transfers between devices with their start and end apart: 4 -> 4, of which waited for: 0 -> 0; matrix products, arithmetic and copies ran while one was open for 0% -> 0% of each run, Pallas kernels for 33% -> 35%
where the time goes in v1:
time: 21.3 us; the launch traced here: 21.1 us
  Pallas kernels  14.7 us (69%)
  starting transfers between devices  5.72 us (27%)
  between operations  0.69 us (3%)
    pallas_call x6, Pallas kernels, call(): pl.pallas_call(kernel, out_shape=tuple(outs), scratch_shapes=list(scratch...  14.7 us
    ppermute x4, starting transfers between devices, swap_with(): return lax.ppermute(message, names, pairs + [(j, i) for i, j in pairs])  5.72 us
  transfers between devices with their start and end apart: 4, of which 0 were waited for; matrix products, arithmetic and copies ran while one was open for 0% of the time, Pallas kernels for 35%

profile of v1, /device:TPU:0, one launch (start us, length us, event | category | flops | bytes accessed | tf_op | source)
XLA Modules:
  0.0 21.1 jit_solution(14060454958958693293)
XLA Ops:
  0.6 2.4 %means_and_message.1 = (f32[4,256,128]{2,1,0:T(8,128)S(1)}, f32[4,256,128]{2,1,0:T(8,128)S(1)}, f32[4,256,128]{2,1,0:T(8,128)S(1)}, f32[4,256,128]{2,1,0:T(8,128...) custom-call(f32[4,256,256]{2,1,0:T(8,128)} %second_hbm.1, ...), custom_call_target="tpu_custom_call" | custom-call | flops 1000000 | bytes 1000000 | tf_op jit(solution)/shard_map/means_and_message/pallas_call | solution.py:1012
  3.1 3.1 %collective-permute-start = (f32[128,128]{1,0:T(8,128)S(1)}, f32[128,128]{1,0:T(8,128)S(1)}, u32[]{:S(2)}, u32[]{:S(2)}) collective-permute-start(f32[128,128]{1,0:T(8,128)S(1)} %get-tuple-element.39), channel_id=1, source_target_pairs={{0,1},{4,5},{8,9},{12,13},{16,17},{20,21},{24,25},{28,29},{2,3},{6... | collective-permute-start | bytes 196616 | tf_op jit(solution)/shard_map/ppermute | solution.py:990
  6.1 0.0 collective-permute-start.1
  6.1 2.0 %whole_terms.1 = (f32[2,4,272,128]{3,2,1,0:T(8,128)S(1)}, f32[2,4,272,128]{3,2,1,0:T(8,128)S(1)}, f32[2,4,272,128]{3,2,1,0:T(8,128)S(1)}, f32[2,2,192,128]{3,2,1...) custom-call(f32[4,256,128]{2,1,0:T(8,128)S(1)} %get-tuple-element.31, ...), custom_call_target="tpu_custom_call" | custom-call | flops 8000000 | bytes 1000000 | tf_op jit(solution)/shard_map/whole_terms/pallas_call | solution.py:1012
  8.2 1.9 %whole_steps.1._whole.whole = f32[2,2,176,128]{3,2,1,0:T(8,128)S(1)} custom-call(f32[2,2,192,128]{3,2,1,0:T(8,128)S(1)} %get-tuple-element.43.initial, f32[2,4,272,128]{3,2,1,0:T(8,128)S(1)} %get-tuple-element.44.offset._wo, f32[2,4,272,128]{3,2,1,0:T(8,128)S(1)} %get-tuple-element.45.grad_rows._wr, f32[2,4,272,128]{3,2,1,0:T(8,128)S(1)} %get-tuple-element.46.grad_cols._wc), custom_call_target="tpu_custom_call" | custom-call | flops 20000000 | bytes 1000000 | tf_op jit(solution)/shard_map/whole_steps/pallas_call | solution.py:1012
  10.0 0.0 collective-permute-done.got_0
  10.1 0.0 collective-permute-done.1.got_1
  10.1 0.3 %row_messages.1 = (f32[144,128]{1,0:T(8,128)S(1)}, f32[144,128]{1,0:T(8,128)S(1)}, f32[128,128]{1,0:T(8,128)S(1)}, f32[128,128]{1,0:T(8,128)S(1)}, f32[8,32,128]{2,1,0:T(8,128)S(1)}) custom-call(f32[256,128]{1,0:T(8,128)S(1)} %get-tuple-element.35.coarse, f32[8,128]{1,0:T(8,128)S(1)} %get-tuple-element.36.own_meta, ...), custom_call_target="tpu_custom_call" | custom-call | flops 1000000 | bytes 1000000 | tf_op jit(solution)/shard_map/row_messages/pallas_call | solution.py:1012
  10.4 2.6 %collective-permute-start.2 = (f32[144,128]{1,0:T(8,128)S(1)}, f32[144,128]{1,0:T(8,128)S(1)}, u32[]{:S(2)}, u32[]{:S(2)}) collective-permute-start(f32[144,128]{1,0:T(8,128)S(1)} %get-tuple-element.53), channel_id=1, source_target_pairs={{4,8},{5,9},{6,10},{7,11},{12,16},{13,17},{14,18},{15,19},{20,24},... | collective-permute-start | bytes 221192 | tf_op jit(solution)/shard_map/ppermute | solution.py:990
  13.0 0.0 collective-permute-start.3
  13.0 3.4 %strip.1 = (f32[2,176,256]{2,1,0:T(8,128)S(1)}, f32[4,256,128]{2,1,0:T(8,128)S(1)}, f32[2,4,8,128]{3,2,1,0:T(8,128)S(1)}, f32[4,272,128]{2,1,0:T(8,128)S(1)}, f3...) custom-call(f32[4,256,128]{2,1,0:T(8,128)S(1)} %get-tuple-element.37.strip_e, ...), custom_call_target="tpu_custom_call" | custom-call | flops 16000000 | bytes 1000000 | tf_op jit(solution)/shard_map/strip/pallas_call | solution.py:1012
  16.4 0.0 collective-permute-done.2.got_1
  16.4 0.0 collective-permute-done.3.got_0
  16.5 4.6 %outer_rows.1 = (f32[2,256,256]{2,1,0:T(8,128)}, f32[2,32,32]{2,1,0:T(8,128)}, f32[2,4,272,128]{3,2,1,0:T(8,128)S(1)}, f32[2,4,272,128]{3,2,1,0:T(8,128)S(1)}, f...) custom-call(f32[4,256,128]{2,1,0:T(8,128)S(1)} %get-tuple-element.31, ...), custom_call_target="tpu_custom_call", output_to_operand_aliasing={{2}: (11, {}), {3}: (12, {}), {4}: (13, {}), {5}: (14, {}),... | custom-call | flops 1000000 | bytes 1000000 | tf_op jit(solution)/shard_map/outer_rows/pallas_call | solution.py:1012
Async XLA Ops:
  3.1 7.0 %collective-permute-start = (f32[128,128]{1,0:T(8,128)S(1)}, f32[128,128]{1,0:T(8,128)S(1)}, u32[]{:S(2)}, u32[]{:S(2)}) collective-permute-start(f32[128,128]{1,0:T(8,128)S(1)} %get-tuple-element.39), channel_id=1, source_target_pairs={{0,1},{4,5},{8,9},{12,13},{16,17},{20,21},{24,25},{28,29},{2,3},{6... | collective-permute-start | bytes 196616 | tf_op jit(solution)/shard_map/ppermute | solution.py:990
  6.1 3.9 %collective-permute-start.1 = (f32[128,128]{1,0:T(8,128)S(1)}, f32[128,128]{1,0:T(8,128)S(1)}, u32[]{:S(2)}, u32[]{:S(2)}) collective-permute-start(f32[128,128]{1,0:T(8,128)S(1)} %get-tuple-element.40), channel_id=1, source_target_pairs={{1,2},{5,6},{9,10},{13,14},{17,18},{21,22},{25,26},{29,30},{0,4},{... | collective-permute-start | bytes 196616 | tf_op jit(solution)/shard_map/ppermute | solution.py:990
  10.4 6.1 %collective-permute-start.2 = (f32[144,128]{1,0:T(8,128)S(1)}, f32[144,128]{1,0:T(8,128)S(1)}, u32[]{:S(2)}, u32[]{:S(2)}) collective-permute-start(f32[144,128]{1,0:T(8,128)S(1)} %get-tuple-element.53), channel_id=1, source_target_pairs={{4,8},{5,9},{6,10},{7,11},{12,16},{13,17},{14,18},{15,19},{20,24},... | collective-permute-start | bytes 221192 | tf_op jit(solution)/shard_map/ppermute | solution.py:990
  13.0 3.5 %collective-permute-start.3 = (f32[144,128]{1,0:T(8,128)S(1)}, f32[144,128]{1,0:T(8,128)S(1)}, u32[]{:S(2)}, u32[]{:S(2)}) collective-permute-start(f32[144,128]{1,0:T(8,128)S(1)} %get-tuple-element.50.own_message), channel_id=1, source_target_pairs={{0,4},{1,5},{2,6},{3,7},{8,12},{9,13},{10,14},{11,15},{16,20},{17,... | collective-permute-start | bytes 221192 | tf_op jit(solution)/shard_map/ppermute | solution.py:990

commit v2 on v1

--- a/solution.py
+++ b/solution.py
@@ -84,12 +84,13 @@
     return jnp.where(place > 0, 1.0, 0.0), jnp.where(place < count - 1, 1.0, 0.0)
 
 
-def shift_at(numbers, row, lane):
-    return numbers[row, lane].astype(jnp.int32), numbers[row, lane + SLOT].astype(jnp.int32)
-
-
-def shifts_of(numbers):
-    return [shift_at(numbers, META - H1, lane) for lane in (0, 80, 48)]
+def shift_at(ref, row, lane):
+    numbers = ref[row : row + 1, :].astype(jnp.int32)
+    return numbers[0, lane], numbers[0, lane + SLOT]
+
+
+def shifts_of(message):
+    return [shift_at(message, META, lane) for lane in (0, 80, 48)]
 
 
 def is_even(axis, like):
@@ -444,7 +445,7 @@
 
 def fine_steps(
     rows_total, chunk, columns, initial, extrap, dual_rows, dual_cols, change, dual_data,
-    offsets, grads_rows, grads_cols, data_row, masks_of, result, kept, done=lambda k: None,
+    offsets, grads_rows, grads_cols, data_row, masks_of, result, kept, done=lambda k: None, first_pulls=None,
 ):
     assert STEPS == 3
     planes = len(offsets)
@@ -507,7 +508,10 @@
                 changes = [change[c, tile, own, :] for c in range(2)]
             pulls = [None, None]
             duals = []
-            for band in range(bands):
+            ready = step == 0 and first_pulls is not None
+            if ready:
+                pulls = [first_pulls[c, tile, own, :] for c in range(2)]
+            for band in range(0 if ready else bands):
                 gradient = (grads_rows[tile][band, data, :], grads_cols[tile][band, data, :])
                 value = offsets[tile][band, data, :]
                 if step > 0:
@@ -571,14 +575,13 @@
 
 def whole_terms_kernel(
     second_0, second_1, first_0, first_1, coarse, own_meta,
-    offset, grad_rows, grad_cols, initial, strip_e, strip_f, up, down, moved, spread, numbers, sem,
+    offset, grad_rows, grad_cols, initial, strip_e, strip_f, up, down, moved, spread,
 ):
     seconds, firsts = (second_0, second_1), (first_0, first_1)
     bands, height, _ = second_0.shape
     block = 120
     coarse_height = coarse.shape[0] // (2 * bands)
-    get_numbers = pltpu.make_async_copy(own_meta, numbers, sem)
-    get_numbers.start()
+    centre = shift_at(own_meta, 0, 0)
     def windows(band, row, rows):
         here = [ref[band, pl.ds(row + centre[0], rows), :].reshape(-1, LANES) for ref in seconds]
         return shift_whole(here, centre[1])
@@ -595,9 +598,6 @@
         strip_e[band, row : row + LANES, :], strip_f[band, row : row + LANES, :] = results
 
     staggered([(band, row) for band in range(bands) for row in range(0, height, LANES)], strips_of, store_strips, 1, woven)
-
-    get_numbers.wait()
-    centre = shift_at(numbers, 0, 0)
 
     ends = [(row, windows(slice(None), row, SUB)) for row in (SUB // 2, height - SUB - SUB // 2)]
     for row, values in ends:
@@ -677,7 +677,7 @@
 def strip_kernel(
     count, strip_e, strip_f, from_left, from_right, wide, own_message, whole,
     middle, strip_out, first_ends, offset, grad_rows, grad_cols,
-    moved, result, spread, numbers, sem, initial, extrap, dual_rows, dual_cols, change, dual_data,
+    moved, result, spread, initial, extrap, dual_rows, dual_cols, change, dual_data,
 ):
     bands, height, _ = strip_e.shape
     block = 120
@@ -685,8 +685,7 @@
     coarse_width = COLUMNS // FACTOR
     rows_total = height - 2 * BEGIN
     lane = lanes_of()
-    get_numbers = pltpu.make_async_copy(own_message.at[pl.ds(H1, SUB), :], numbers, sem)
-    get_numbers.start()
+    centre, right, left = shifts_of(own_message)
     has_left, has_right = neighbours("col", count)
     exists = jnp.where(lane < S_RIGHT, 1.0, jnp.where(lane < S_LEFT, has_right, has_left))
 
@@ -721,9 +720,6 @@
     firsts = [(end, band, first_of(band, (0, height - SUB)[end], SUB)) for end in range(2) for band in range(bands)]
     for end, band, value in firsts:
         first_ends[end, band] = value
-
-    get_numbers.wait()
-    centre, right, left = shifts_of(numbers)
 
     def windows(band, row, rows):
         return strip_windows(
@@ -787,7 +783,7 @@
     counts, second_0, second_1, first_0, first_1, strip_e, first_ends, wide, got_1, got_0, middle, own_message,
     _wo, _wr, _wc, _so, _sr, _sc,
     flow_out, coarse_out, whole_offset, whole_rows, whole_cols, strip_offset, strip_rows, strip_cols,
-    from_up, from_down, extended, tall, spread, masks, result, joined, coarse_result, numbers, sems,
+    from_up, from_down, extended, tall, spread, masks, result, joined, coarse_result, pulls, sems,
     initial, extrap, dual_rows, dual_cols, change, dual_data,
 ):
     bands, height, _ = second_0.shape
@@ -802,12 +798,13 @@
         sems.at[0],
     )
     put_middle.start()
-    get_numbers = [
-        pltpu.make_async_copy(message.at[pl.ds(H1, SUB), :], numbers.at[k], sems.at[4 + k])
-        for k, message in enumerate((own_message, got_0, got_1))
-    ]
-    for get in get_numbers:
-        get.start()
+    own, one, other = [shifts_of(message) for message in (own_message, got_0, got_1)]
+    odd = lax.axis_index("row") % 2
+
+    def of_row(for_even, for_odd):
+        return [tuple(jnp.where(odd == 0, x, y) for x, y in zip(*pair)) for pair in zip(for_even, for_odd)]
+
+    above, below = of_row(other, one), of_row(one, other)
 
     other = without_ends(got_1, "row", counts[0])
     even = is_even("row", got_0)
@@ -854,16 +851,6 @@
     rows_data = whole_offset.shape[2]
     exists_tall = jnp.concatenate([exists] * bands, axis=0)
 
-    for get in get_numbers:
-        get.wait()
-    own, one, other = [shifts_of(numbers.at[k]) for k in range(3)]
-    odd = lax.axis_index("row") % 2
-
-    def of_row(for_even, for_odd):
-        return [tuple(jnp.where(odd == 0, x, y) for x, y in zip(*pair)) for pair in zip(for_even, for_odd)]
-
-    above, below = of_row(other, one), of_row(one, other)
-
     def rows_of(halo, end):
         if halo:
             return slice(0, SUB) if end == 0 else slice(rows_data - SUB, rows_data)
@@ -920,6 +907,28 @@
 
     staggered([(halo, end) for halo in (True, False) for end in range(2)], values_of, store_values, 1, woven)
 
+    def data_row(k):
+        return k * (rows_data - EACH)
+
+    offsets = [whole_offset.at[0], whole_offset.at[1], strip_offset]
+    grads_rows = [whole_rows.at[0], whole_rows.at[1], strip_rows]
+    grads_cols = [whole_cols.at[0], whole_cols.at[1], strip_cols]
+
+    def pulls_of(item):
+        k, tile = item
+        data = pl.ds(data_row(k), EACH)
+        duals = [jnp.clip(offsets[tile][band, data, :], -UNIT * LIMIT, UNIT * LIMIT) for band in range(bands)]
+        return [
+            sum(duals[band] * grads[tile][band, data, :] for band in range(bands)) for grads in (grads_rows, grads_cols)
+        ]
+
+    def store_pulls(item, values):
+        k, tile = item
+        for c in range(2):
+            pulls[c, tile, k * EACH : (k + 1) * EACH, :] = values[c]
+
+    staggered([(k, tile) for k in range(2) for tile in range(3)], pulls_of, store_pulls, 1, woven)
+
     flow = woven.finish()
     for c in range(2):
         coarse_result[c] = turn(flow[c][LEAD : LEAD + coarse_height], -LEAD)[:, :coarse_width]
@@ -955,16 +964,10 @@
         join(result, result.at[:, 2], joined, slice(k * EACH + SUB, k * EACH + SUB + MARGIN))
         puts[k].start()
 
-    def data_row(k):
-        return k * (rows_data - EACH)
-
     fine_steps(
         rows_total, chunk, lambda fields: columns_whole(fields[:2], edges) + [columns_strip(fields[2])],
         initial, extrap, dual_rows, dual_cols, change, dual_data,
-        [whole_offset.at[0], whole_offset.at[1], strip_offset],
-        [whole_rows.at[0], whole_rows.at[1], strip_rows],
-        [whole_cols.at[0], whole_cols.at[1], strip_cols],
-        data_row, masks_of, result, lambda k: (SUB, SUB), finish,
+        offsets, grads_rows, grads_cols, data_row, masks_of, result, lambda k: (SUB, SUB), finish, pulls,
     )
     put_middle.wait()
     put_coarse.wait()
@@ -1050,7 +1053,6 @@
         ],
         [
             scratch(2, bands, height, LANES), scratch(2, 2, coarse_height, LANES),
-            pltpu.SMEM((SUB, LANES), jnp.float32), pltpu.SemaphoreType.DMA,
         ],
         flops=8_000_000,
     )
@@ -1081,8 +1083,6 @@
             scratch(bands, height, LANES),
             scratch(2, 1, inner_rows, LANES),
             scratch(2, 1, coarse_height, LANES),
-            pltpu.SMEM((SUB, LANES), jnp.float32),
-            pltpu.SemaphoreType.DMA,
             *fine_scratch(bands, 1, inner_rows),
         ],
         flops=16_000_000,
@@ -1106,8 +1106,8 @@
             scratch(2, 3, 2 * EACH, LANES),
             scratch(2, 2 * EACH, width),
             scratch(2, coarse_height, coarse_width),
-            pltpu.SMEM((3, SUB, LANES), jnp.float32),
-            pltpu.SemaphoreType.DMA((7,)),
+            scratch(2, 3, 2 * EACH, LANES),
+            pltpu.SemaphoreType.DMA((4,)),
             *fine_scratch(bands, 3, 2 * EACH),
         ],
         out_specs=(hbm, hbm) + (vmem,) * 6,

time: 21.3 us -> 19.8 us (0.930)
  Pallas kernels: 14.7 us -> 13.2 us
    pallas_call x6, Pallas kernels: 14.7 us -> 13.2 us  [call(): pl.pallas_call(kernel, out_shape=tuple(outs), scratch_shapes=list(scratch...]
  transfers between devices with their start and end apart: 4 -> 4, of which waited for: 0 -> 0; matrix products, arithmetic and copies ran while one was open for 0% -> 0% of each run, Pallas kernels for 35% -> 33%
where the time goes in v2:
time: 19.8 us; the launch traced here: 19.6 us
  Pallas kernels  13.2 us (67%)
  starting transfers between devices  5.72 us (29%)
  between operations  0.68 us (3%)
    pallas_call x6, Pallas kernels, call(): pl.pallas_call(kernel, out_shape=tuple(outs), scratch_shapes=list(scratch...  13.2 us
    ppermute x4, starting transfers between devices, swap_with(): return lax.ppermute(message, names, pairs + [(j, i) for i, j in pairs])  5.72 us
  transfers between devices with their start and end apart: 4, of which 0 were waited for; matrix products, arithmetic and copies ran while one was open for 0% of the time, Pallas kernels for 33%

profile of v2, /device:TPU:0, one launch (start us, length us, event | category | flops | bytes accessed | tf_op | source)
XLA Modules:
  0.0 19.6 jit_solution(17755237921483115644)
XLA Ops:
  0.6 2.4 %means_and_message.1 = (f32[4,256,128]{2,1,0:T(8,128)S(1)}, f32[4,256,128]{2,1,0:T(8,128)S(1)}, f32[4,256,128]{2,1,0:T(8,128)S(1)}, f32[4,256,128]{2,1,0:T(8,128...) custom-call(f32[4,256,256]{2,1,0:T(8,128)} %second_hbm.1, ...), custom_call_target="tpu_custom_call" | custom-call | flops 1000000 | bytes 1000000 | tf_op jit(solution)/shard_map/means_and_message/pallas_call | solution.py:1015
  3.1 3.1 %collective-permute-start = (f32[128,128]{1,0:T(8,128)S(1)}, f32[128,128]{1,0:T(8,128)S(1)}, u32[]{:S(2)}, u32[]{:S(2)}) collective-permute-start(f32[128,128]{1,0:T(8,128)S(1)} %get-tuple-element.39), channel_id=1, source_target_pairs={{0,1},{4,5},{8,9},{12,13},{16,17},{20,21},{24,25},{28,29},{2,3},{6... | collective-permute-start | bytes 196616 | tf_op jit(solution)/shard_map/ppermute | solution.py:993
  6.1 0.0 collective-permute-start.1
  6.1 1.8 %whole_terms.1 = (f32[2,4,272,128]{3,2,1,0:T(8,128)S(1)}, f32[2,4,272,128]{3,2,1,0:T(8,128)S(1)}, f32[2,4,272,128]{3,2,1,0:T(8,128)S(1)}, f32[2,2,192,128]{3,2,1...) custom-call(f32[4,256,128]{2,1,0:T(8,128)S(1)} %get-tuple-element.31, ...), custom_call_target="tpu_custom_call" | custom-call | flops 8000000 | bytes 1000000 | tf_op jit(solution)/shard_map/whole_terms/pallas_call | solution.py:1015
  7.9 1.9 %whole_steps.1._whole.whole = f32[2,2,176,128]{3,2,1,0:T(8,128)S(1)} custom-call(f32[2,2,192,128]{3,2,1,0:T(8,128)S(1)} %get-tuple-element.43.initial, f32[2,4,272,128]{3,2,1,0:T(8,128)S(1)} %get-tuple-element.44.offset._wo, f32[2,4,272,128]{3,2,1,0:T(8,128)S(1)} %get-tuple-element.45.grad_rows._wr, f32[2,4,272,128]{3,2,1,0:T(8,128)S(1)} %get-tuple-element.46.grad_cols._wc), custom_call_target="tpu_custom_call" | custom-call | flops 20000000 | bytes 1000000 | tf_op jit(solution)/shard_map/whole_steps/pallas_call | solution.py:1015
  9.8 0.0 collective-permute-done.got_0
  9.8 0.0 collective-permute-done.1.got_1
  9.8 0.3 %row_messages.1 = (f32[144,128]{1,0:T(8,128)S(1)}, f32[144,128]{1,0:T(8,128)S(1)}, f32[128,128]{1,0:T(8,128)S(1)}, f32[128,128]{1,0:T(8,128)S(1)}, f32[8,32,128]{2,1,0:T(8,128)S(1)}) custom-call(f32[256,128]{1,0:T(8,128)S(1)} %get-tuple-element.35.coarse, f32[8,128]{1,0:T(8,128)S(1)} %get-tuple-element.36.own_meta, ...), custom_call_target="tpu_custom_call" | custom-call | flops 1000000 | bytes 1000000 | tf_op jit(solution)/shard_map/row_messages/pallas_call | solution.py:1015
  10.1 2.6 %collective-permute-start.2 = (f32[144,128]{1,0:T(8,128)S(1)}, f32[144,128]{1,0:T(8,128)S(1)}, u32[]{:S(2)}, u32[]{:S(2)}) collective-permute-start(f32[144,128]{1,0:T(8,128)S(1)} %get-tuple-element.53), channel_id=1, source_target_pairs={{4,8},{5,9},{6,10},{7,11},{12,16},{13,17},{14,18},{15,19},{20,24},... | collective-permute-start | bytes 221192 | tf_op jit(solution)/shard_map/ppermute | solution.py:993
  12.7 0.0 collective-permute-start.3
  12.7 2.9 %strip.1 = (f32[2,176,256]{2,1,0:T(8,128)S(1)}, f32[4,256,128]{2,1,0:T(8,128)S(1)}, f32[2,4,8,128]{3,2,1,0:T(8,128)S(1)}, f32[4,272,128]{2,1,0:T(8,128)S(1)}, f3...) custom-call(f32[4,256,128]{2,1,0:T(8,128)S(1)} %get-tuple-element.37.strip_e, ...), custom_call_target="tpu_custom_call" | custom-call | flops 16000000 | bytes 1000000 | tf_op jit(solution)/shard_map/strip/pallas_call | solution.py:1015
  15.6 0.0 collective-permute-done.2.got_1
  15.6 0.0 collective-permute-done.3.got_0
  15.6 4.0 %outer_rows.1 = (f32[2,256,256]{2,1,0:T(8,128)}, f32[2,32,32]{2,1,0:T(8,128)}, f32[2,4,272,128]{3,2,1,0:T(8,128)S(1)}, f32[2,4,272,128]{3,2,1,0:T(8,128)S(1)}, f...) custom-call(f32[4,256,128]{2,1,0:T(8,128)S(1)} %get-tuple-element.31, ...), custom_call_target="tpu_custom_call", output_to_operand_aliasing={{2}: (11, {}), {3}: (12, {}), {4}: (13, {}), {5}: (14, {}),... | custom-call | flops 1000000 | bytes 1000000 | tf_op jit(solution)/shard_map/outer_rows/pallas_call | solution.py:1015
Async XLA Ops:
  3.1 6.7 %collective-permute-start = (f32[128,128]{1,0:T(8,128)S(1)}, f32[128,128]{1,0:T(8,128)S(1)}, u32[]{:S(2)}, u32[]{:S(2)}) collective-permute-start(f32[128,128]{1,0:T(8,128)S(1)} %get-tuple-element.39), channel_id=1, source_target_pairs={{0,1},{4,5},{8,9},{12,13},{16,17},{20,21},{24,25},{28,29},{2,3},{6... | collective-permute-start | bytes 196616 | tf_op jit(solution)/shard_map/ppermute | solution.py:993
  6.1 3.7 %collective-permute-start.1 = (f32[128,128]{1,0:T(8,128)S(1)}, f32[128,128]{1,0:T(8,128)S(1)}, u32[]{:S(2)}, u32[]{:S(2)}) collective-permute-start(f32[128,128]{1,0:T(8,128)S(1)} %get-tuple-element.40), channel_id=1, source_target_pairs={{1,2},{5,6},{9,10},{13,14},{17,18},{21,22},{25,26},{29,30},{0,4},{... | collective-permute-start | bytes 196616 | tf_op jit(solution)/shard_map/ppermute | solution.py:993
  10.1 5.5 %collective-permute-start.2 = (f32[144,128]{1,0:T(8,128)S(1)}, f32[144,128]{1,0:T(8,128)S(1)}, u32[]{:S(2)}, u32[]{:S(2)}) collective-permute-start(f32[144,128]{1,0:T(8,128)S(1)} %get-tuple-element.53), channel_id=1, source_target_pairs={{4,8},{5,9},{6,10},{7,11},{12,16},{13,17},{14,18},{15,19},{20,24},... | collective-permute-start | bytes 221192 | tf_op jit(solution)/shard_map/ppermute | solution.py:993
  12.7 2.9 %collective-permute-start.3 = (f32[144,128]{1,0:T(8,128)S(1)}, f32[144,128]{1,0:T(8,128)S(1)}, u32[]{:S(2)}, u32[]{:S(2)}) collective-permute-start(f32[144,128]{1,0:T(8,128)S(1)} %get-tuple-element.50.own_message), channel_id=1, source_target_pairs={{0,4},{1,5},{2,6},{3,7},{8,12},{9,13},{10,14},{11,15},{16,20},{17,... | collective-permute-start | bytes 221192 | tf_op jit(solution)/shard_map/ppermute | solution.py:993

commit v3 on v2

--- a/solution.py
+++ b/solution.py
@@ -445,7 +445,7 @@
 
 def fine_steps(
     rows_total, chunk, columns, initial, extrap, dual_rows, dual_cols, change, dual_data,
-    offsets, grads_rows, grads_cols, data_row, masks_of, result, kept, done=lambda k: None, first_pulls=None,
+    offsets, grads_rows, grads_cols, data_row, masks_of, result, kept, done=lambda k: None, first_pulls=None, depth=1,
 ):
     assert STEPS == 3
     planes = len(offsets)
@@ -490,7 +490,7 @@
                 dual_rows[c, tile, places(k)[0], :] = rows
                 dual_cols[c, tile, places(k)[1], :] = cols
 
-        staggered([(k, c) for k in range(chunks) for c in range(2)], dual, store_dual, 1)
+        staggered([(k, c) for k in range(chunks) for c in range(2)], dual, store_dual, depth)
         along_of = {}
 
         def primal(item, step=step, final=final, along_of=along_of):
@@ -549,7 +549,7 @@
                 for band in range(bands):
                     dual_data[band, tile, own, :] = duals[band]
 
-        staggered([(k, tile) for k in range(chunks) for tile in tiles], primal, store_primal, 1)
+        staggered([(k, tile) for k in range(chunks) for tile in tiles], primal, store_primal, depth)
 
 
 def clear_guards(*refs):
@@ -664,13 +664,14 @@
 ):
     rows_total = result.shape[2]
     clear_guards(extrap, dual_rows)
-    chunk = 88
+    chunk = 16
     edges = {}
     fine_steps(
         rows_total, chunk, lambda fields: columns_whole(fields, edges),
         initial, extrap, dual_rows, dual_cols, change, dual_data,
         *[[ref.at[tile] for tile in range(2)] for ref in (offset, grad_rows, grad_cols)],
-        lambda k: HALO + BEGIN + k * chunk, lambda own: (1.0, 1.0), result, lambda k: (SUB * (k == 0), SUB * (k == 1)),
+        lambda k: HALO + BEGIN + k * chunk, lambda own: (1.0, 1.0), result,
+        lambda k: (SUB * (k == 0), SUB * (k == rows_total // chunk - 1)), depth=3,
     )
 
 
@@ -758,12 +759,13 @@
     clear_guards(initial, extrap, dual_rows)
     repeat_rows(spread, initial, [BEGIN // FACTOR + k for k in range(rows_total // SUB)])
 
-    chunk = 176
+    chunk = 88
     masks = jnp.concatenate([exists] * (chunk // SUB), axis=0)
     fine_steps(
         rows_total, chunk, lambda fields: [columns_strip(fields[0])],
         initial, extrap, dual_rows, dual_cols, change, dual_data, [offset], [grad_rows], [grad_cols],
-        lambda k: HALO + BEGIN + k * chunk, lambda own: (masks[: own.size],), result, lambda k: (SUB, SUB),
+        lambda k: HALO + BEGIN + k * chunk, lambda own: (masks[: own.size],), result,
+        lambda k: (SUB * (k == 0), SUB * (k == rows_total // chunk - 1)),
     )
     join(whole, result.at[:, 0], middle, slice(SUB, rows_total - SUB))
 
@@ -908,7 +910,7 @@
     staggered([(halo, end) for halo in (True, False) for end in range(2)], values_of, store_values, 1, woven)
 
     def data_row(k):
-        return k * (rows_data - EACH)
+        return k // 2 * (rows_data - EACH) + k % 2 * (EACH // 2)
 
     offsets = [whole_offset.at[0], whole_offset.at[1], strip_offset]
     grads_rows = [whole_rows.at[0], whole_rows.at[1], strip_rows]
@@ -916,7 +918,7 @@
 
     def pulls_of(item):
         k, tile = item
-        data = pl.ds(data_row(k), EACH)
+        data = pl.ds(data_row(2 * k), EACH)
         duals = [jnp.clip(offsets[tile][band, data, :], -UNIT * LIMIT, UNIT * LIMIT) for band in range(bands)]
         return [
             sum(duals[band] * grads[tile][band, data, :] for band in range(bands)) for grads in (grads_rows, grads_cols)
@@ -949,7 +951,7 @@
         whole = masks[0, rows, :]
         return (whole, whole, masks[1, rows, :])
 
-    chunk = EACH
+    chunk = EACH // 2
     edges = {}
     puts = [
         pltpu.make_async_copy(
@@ -961,13 +963,16 @@
     ]
 
     def finish(k):
-        join(result, result.at[:, 2], joined, slice(k * EACH + SUB, k * EACH + SUB + MARGIN))
-        puts[k].start()
+        if k % 2 == 1:
+            at = k // 2 * EACH + SUB
+            join(result, result.at[:, 2], joined, slice(at, at + MARGIN))
+            puts[k // 2].start()
 
     fine_steps(
         rows_total, chunk, lambda fields: columns_whole(fields[:2], edges) + [columns_strip(fields[2])],
         initial, extrap, dual_rows, dual_cols, change, dual_data,
-        offsets, grads_rows, grads_cols, data_row, masks_of, result, lambda k: (SUB, SUB), finish, pulls,
+        offsets, grads_rows, grads_cols, data_row, masks_of, result,
+        lambda k: (SUB, 0) if k % 2 == 0 else (0, SUB), finish, pulls, depth=2,
     )
     put_middle.wait()
     put_coarse.wait()

time: 19.8 us -> 19.6 us (0.990)
  Pallas kernels: 13.2 us -> 12.9 us
    pallas_call x6, Pallas kernels: 13.2 us -> 12.9 us  [call(): pl.pallas_call(kernel, out_shape=tuple(outs), scratch_shapes=list(scratch...]
where the time goes in v3:
time: 19.6 us; the launch traced here: 19.3 us
  Pallas kernels  12.9 us (66%)
  starting transfers between devices  5.71 us (29%)
  between operations  0.68 us (3%)
    pallas_call x6, Pallas kernels, call(): pl.pallas_call(kernel, out_shape=tuple(outs), scratch_shapes=list(scratch...  12.9 us
    ppermute x4, starting transfers between devices, swap_with(): return lax.ppermute(message, names, pairs + [(j, i) for i, j in pairs])  5.71 us
  transfers between devices with their start and end apart: 4, of which 0 were waited for; matrix products, arithmetic and copies ran while one was open for 0% of the time, Pallas kernels for 33%

profile of v3, /device:TPU:0, one launch (start us, length us, event | category | flops | bytes accessed | tf_op | source)
XLA Modules:
  0.0 19.3 jit_solution(7854956575357152997)
XLA Ops:
  0.6 2.4 %means_and_message.1 = (f32[4,256,128]{2,1,0:T(8,128)S(1)}, f32[4,256,128]{2,1,0:T(8,128)S(1)}, f32[4,256,128]{2,1,0:T(8,128)S(1)}, f32[4,256,128]{2,1,0:T(8,128...) custom-call(f32[4,256,256]{2,1,0:T(8,128)} %second_hbm.1, ...), custom_call_target="tpu_custom_call" | custom-call | flops 1000000 | bytes 1000000 | tf_op jit(solution)/shard_map/means_and_message/pallas_call | solution.py:1020
  3.1 3.1 %collective-permute-start = (f32[128,128]{1,0:T(8,128)S(1)}, f32[128,128]{1,0:T(8,128)S(1)}, u32[]{:S(2)}, u32[]{:S(2)}) collective-permute-start(f32[128,128]{1,0:T(8,128)S(1)} %get-tuple-element.39), channel_id=1, source_target_pairs={{0,1},{4,5},{8,9},{12,13},{16,17},{20,21},{24,25},{28,29},{2,3},{6... | collective-permute-start | bytes 196616 | tf_op jit(solution)/shard_map/ppermute | solution.py:998
  6.1 0.0 collective-permute-start.1
  6.1 1.8 %whole_terms.1 = (f32[2,4,272,128]{3,2,1,0:T(8,128)S(1)}, f32[2,4,272,128]{3,2,1,0:T(8,128)S(1)}, f32[2,4,272,128]{3,2,1,0:T(8,128)S(1)}, f32[2,2,192,128]{3,2,1...) custom-call(f32[4,256,128]{2,1,0:T(8,128)S(1)} %get-tuple-element.31, ...), custom_call_target="tpu_custom_call" | custom-call | flops 8000000 | bytes 1000000 | tf_op jit(solution)/shard_map/whole_terms/pallas_call | solution.py:1020
  7.9 1.7 %whole_steps.1._whole.whole = f32[2,2,176,128]{3,2,1,0:T(8,128)S(1)} custom-call(f32[2,2,192,128]{3,2,1,0:T(8,128)S(1)} %get-tuple-element.43.initial, f32[2,4,272,128]{3,2,1,0:T(8,128)S(1)} %get-tuple-element.44.offset._wo, f32[2,4,272,128]{3,2,1,0:T(8,128)S(1)} %get-tuple-element.45.grad_rows._wr, f32[2,4,272,128]{3,2,1,0:T(8,128)S(1)} %get-tuple-element.46.grad_cols._wc), custom_call_target="tpu_custom_call" | custom-call | flops 20000000 | bytes 1000000 | tf_op jit(solution)/shard_map/whole_steps/pallas_call | solution.py:1020
  9.6 0.0 collective-permute-done.got_0
  9.7 0.0 collective-permute-done.1.got_1
  9.7 0.3 %row_messages.1 = (f32[144,128]{1,0:T(8,128)S(1)}, f32[144,128]{1,0:T(8,128)S(1)}, f32[128,128]{1,0:T(8,128)S(1)}, f32[128,128]{1,0:T(8,128)S(1)}, f32[8,32,128]{2,1,0:T(8,128)S(1)}) custom-call(f32[256,128]{1,0:T(8,128)S(1)} %get-tuple-element.35.coarse, f32[8,128]{1,0:T(8,128)S(1)} %get-tuple-element.36.own_meta, ...), custom_call_target="tpu_custom_call" | custom-call | flops 1000000 | bytes 1000000 | tf_op jit(solution)/shard_map/row_messages/pallas_call | solution.py:1020
  9.9 2.6 %collective-permute-start.2 = (f32[144,128]{1,0:T(8,128)S(1)}, f32[144,128]{1,0:T(8,128)S(1)}, u32[]{:S(2)}, u32[]{:S(2)}) collective-permute-start(f32[144,128]{1,0:T(8,128)S(1)} %get-tuple-element.53), channel_id=1, source_target_pairs={{4,8},{5,9},{6,10},{7,11},{12,16},{13,17},{14,18},{15,19},{20,24},... | collective-permute-start | bytes 221192 | tf_op jit(solution)/shard_map/ppermute | solution.py:998
  12.6 0.0 collective-permute-start.3
  12.6 2.8 %strip.1 = (f32[2,176,256]{2,1,0:T(8,128)S(1)}, f32[4,256,128]{2,1,0:T(8,128)S(1)}, f32[2,4,8,128]{3,2,1,0:T(8,128)S(1)}, f32[4,272,128]{2,1,0:T(8,128)S(1)}, f3...) custom-call(f32[4,256,128]{2,1,0:T(8,128)S(1)} %get-tuple-element.37.strip_e, ...), custom_call_target="tpu_custom_call" | custom-call | flops 16000000 | bytes 1000000 | tf_op jit(solution)/shard_map/strip/pallas_call | solution.py:1020
  15.4 0.0 collective-permute-done.2.got_1
  15.4 0.0 collective-permute-done.3.got_0
  15.4 3.9 %outer_rows.1 = (f32[2,256,256]{2,1,0:T(8,128)}, f32[2,32,32]{2,1,0:T(8,128)}, f32[2,4,272,128]{3,2,1,0:T(8,128)S(1)}, f32[2,4,272,128]{3,2,1,0:T(8,128)S(1)}, f...) custom-call(f32[4,256,128]{2,1,0:T(8,128)S(1)} %get-tuple-element.31, ...), custom_call_target="tpu_custom_call", output_to_operand_aliasing={{2}: (11, {}), {3}: (12, {}), {4}: (13, {}), {5}: (14, {}),... | custom-call | flops 1000000 | bytes 1000000 | tf_op jit(solution)/shard_map/outer_rows/pallas_call | solution.py:1020
Async XLA Ops:
  3.1 6.6 %collective-permute-start = (f32[128,128]{1,0:T(8,128)S(1)}, f32[128,128]{1,0:T(8,128)S(1)}, u32[]{:S(2)}, u32[]{:S(2)}) collective-permute-start(f32[128,128]{1,0:T(8,128)S(1)} %get-tuple-element.39), channel_id=1, source_target_pairs={{0,1},{4,5},{8,9},{12,13},{16,17},{20,21},{24,25},{28,29},{2,3},{6... | collective-permute-start | bytes 196616 | tf_op jit(solution)/shard_map/ppermute | solution.py:998
  6.1 3.5 %collective-permute-start.1 = (f32[128,128]{1,0:T(8,128)S(1)}, f32[128,128]{1,0:T(8,128)S(1)}, u32[]{:S(2)}, u32[]{:S(2)}) collective-permute-start(f32[128,128]{1,0:T(8,128)S(1)} %get-tuple-element.40), channel_id=1, source_target_pairs={{1,2},{5,6},{9,10},{13,14},{17,18},{21,22},{25,26},{29,30},{0,4},{... | collective-permute-start | bytes 196616 | tf_op jit(solution)/shard_map/ppermute | solution.py:998
  9.9 5.4 %collective-permute-start.2 = (f32[144,128]{1,0:T(8,128)S(1)}, f32[144,128]{1,0:T(8,128)S(1)}, u32[]{:S(2)}, u32[]{:S(2)}) collective-permute-start(f32[144,128]{1,0:T(8,128)S(1)} %get-tuple-element.53), channel_id=1, source_target_pairs={{4,8},{5,9},{6,10},{7,11},{12,16},{13,17},{14,18},{15,19},{20,24},... | collective-permute-start | bytes 221192 | tf_op jit(solution)/shard_map/ppermute | solution.py:998
  12.6 2.8 %collective-permute-start.3 = (f32[144,128]{1,0:T(8,128)S(1)}, f32[144,128]{1,0:T(8,128)S(1)}, u32[]{:S(2)}, u32[]{:S(2)}) collective-permute-start(f32[144,128]{1,0:T(8,128)S(1)} %get-tuple-element.50.own_message), channel_id=1, source_target_pairs={{0,4},{1,5},{2,6},{3,7},{8,12},{9,13},{10,14},{11,15},{16,20},{17,... | collective-permute-start | bytes 221192 | tf_op jit(solution)/shard_map/ppermute | solution.py:998
